TPU v7x, 32 devices: a whole 2x2x4 slice. The times are simulated.
32 devices in a mesh: ctx: 8 (over z, x), head: 4 (over y, core).
Axes of the slice: x: 2, y: 2, z: 4, core: 2. Of those that a mesh axis runs over, the one named last changes fastest.
Arguments:
- queries: bfloat16 [2048, 8, 128], P('ctx', 'head'), may hold values from -6 to 6
- spikes: int32 [2048, 8, 128], P('ctx', 'head'), may hold values from 0 to 3
- values: bfloat16 [2048, 8, 128], P('ctx', 'head'), may hold values from -6 to 6
- threshold: float32 [128], replicated, may hold values from 0.05 to 0.5
- norm_gain: float32 [128], replicated, may hold values from 0.1 to 1.9
- document_ids: int32 [2048], P('ctx'), may hold values from 0 to 31, never falling along the last dimension, each value on 1 to 512 neighbouring positions
- cotangent: bfloat16 [2048, 8, 128], P('ctx', 'head'), may hold values from -6 to 6
Outputs:
- attended: bfloat16 [2048, 8, 128], P('ctx', 'head')
- query_grad: bfloat16 [2048, 8, 128], P('ctx', 'head')
- value_grad: bfloat16 [2048, 8, 128], P('ctx', 'head')
- threshold_grad: float32 [128], replicated
- gain_grad: float32 [128], replicated
Inputs may be any that keep to these rules, and one draw needn't show every extreme that they name: `document_ids`: ids never fall along the context; each document holds 1 to 512 consecutive tokens, and one holds exactly 512.
All inputs are finite; a program needn't handle non-finite values.
Results may differ from a plain program's by a relative error of at most 0.011.
Values sent between devices are 32-bit elements; how exact they have to be, the bound alone decides.
No kernel may reach another device: no remote copies, remote signals or barrier semaphores. Data moves between devices by JAX's collectives and lax.ppermute only.
A program may use at most 128 MiB of HBM per device.

v0:
```python
import math

import jax
import jax.numpy as jnp
from jax import lax
from jax.sharding import PartitionSpec as P


def entering(value, axis, join, neutral, backward):
    count, mine = (lax.axis_size(axis), lax.axis_index(axis))
    pieces = jax.tree.map(lambda part: lax.all_gather(part, axis), value)
    if backward:
        pieces = jax.tree.map(lambda part: part[::-1], pieces)
        mine = count - 1 - mine
    so_far = jax.tree.map(
        lambda part, zero: jnp.full_like(part, 0) + jnp.asarray(zero, part.dtype), value, neutral
    )

    def step(position, so_far):
        longer = join(so_far, jax.tree.map(lambda part: part[position], pieces))
        return jax.tree.map(lambda new, old: jnp.where(position < mine, new, old), longer, so_far)

    return lax.fori_loop(0, count - 1, step, so_far)


def join_states(earlier, later):
    early_state, early_mark = earlier
    later_state, later_mark = later
    empty_later = later_mark < 0
    keeping = jnp.logical_or(early_mark == later_mark, empty_later).astype(jnp.float32)
    joined = later_state + keeping * early_state
    return (joined, jnp.where(empty_later, early_mark, later_mark))


def on_device(queries, spikes, values, threshold, norm_gain, document_ids, cotangent):
    length = queries.shape[0]
    head_count = queries.shape[1]
    width = queries.shape[2]
    keys_bf = (spikes.astype(jnp.float32) * threshold).astype(jnp.bfloat16)
    position = jnp.arange(length, dtype=jnp.int32)
    allowed = (position[None, :] <= position[:, None]) & (
        document_ids[:, None] == document_ids[None, :]
    )
    head_doc = document_ids[0]
    tail_doc = document_ids[-1]
    first_mask = document_ids == head_doc
    last_mask = document_ids == tail_doc
    first_bf = first_mask.astype(jnp.bfloat16)[:, None, None]
    last_bf = last_mask.astype(jnp.bfloat16)[:, None, None]
    first_f32 = first_mask.astype(jnp.float32)[:, None, None]
    last_f32 = last_mask.astype(jnp.float32)[:, None, None]
    zero_state = jnp.zeros((head_count, width, width), jnp.float32)
    identity = (zero_state, jnp.float32(-1.0))
    tail = jnp.einsum("thd,the->hde", keys_bf * last_bf, values, preferred_element_type=jnp.float32)
    before, before_mark = entering(
        (tail, tail_doc.astype(jnp.float32)), "ctx", join_states, identity, False
    )
    carried = jnp.where(before_mark == head_doc.astype(jnp.float32), before, 0.0).astype(
        jnp.bfloat16
    )
    raw_scores = jnp.einsum("shd,thd->hst", queries, keys_bf, preferred_element_type=jnp.float32)
    scores = jnp.where(allowed[None], raw_scores, 0.0).astype(jnp.bfloat16)
    inside = jnp.einsum("hst,thd->shd", scores, values, preferred_element_type=jnp.float32)
    mixed_raw = (
        queries.astype(jnp.float32)
        + inside
        + first_f32
        * jnp.einsum("shd,hde->she", queries, carried, preferred_element_type=jnp.float32)
    )
    ratio = lax.rsqrt(jnp.mean(mixed_raw * mixed_raw, axis=-1, keepdims=True) + 1e-06)
    normed = mixed_raw * ratio
    attended = (normed * norm_gain).astype(jnp.bfloat16)
    cot_f = cotangent.astype(jnp.float32)
    upstream = cot_f * norm_gain
    gnorm = (
        ratio * upstream - normed * ratio * jnp.mean(normed * upstream, axis=-1, keepdims=True)
    ).astype(jnp.bfloat16)
    gain_term = jnp.sum(cot_f * normed, axis=(0, 1))
    raw_dscores = jnp.einsum("shd,thd->hst", gnorm, values, preferred_element_type=jnp.float32)
    dscores = jnp.where(allowed[None], raw_dscores, 0.0).astype(jnp.bfloat16)
    tail_back = jnp.einsum(
        "shd,she->hde", queries * first_bf, gnorm, preferred_element_type=jnp.float32
    )
    after, after_mark = entering(
        (tail_back, head_doc.astype(jnp.float32)), "ctx", join_states, identity, True
    )
    returned = jnp.where(after_mark == tail_doc.astype(jnp.float32), after, 0.0).astype(
        jnp.bfloat16
    )
    query_grad = gnorm.astype(jnp.float32) + jnp.einsum(
        "hst,thd->shd", dscores, keys_bf, preferred_element_type=jnp.float32
    )
    query_grad = query_grad + first_f32 * jnp.einsum(
        "she,hde->shd", gnorm, carried, preferred_element_type=jnp.float32
    )
    key_grad = jnp.einsum("hst,shd->thd", dscores, queries, preferred_element_type=jnp.float32)
    key_grad = key_grad + last_f32 * jnp.einsum(
        "the,hde->thd", values, returned, preferred_element_type=jnp.float32
    )
    value_grad = jnp.einsum("hst,she->the", scores, gnorm, preferred_element_type=jnp.float32)
    value_grad = value_grad + last_f32 * jnp.einsum(
        "thd,hde->the", keys_bf, returned, preferred_element_type=jnp.float32
    )
    thresh_term = jnp.sum(spikes.astype(jnp.float32) * key_grad, axis=(0, 1))
    totals = lax.psum((thresh_term, gain_term), ("ctx", "head"))
    scale = 1.0 / math.sqrt(length * lax.axis_size("ctx") * head_count * lax.axis_size("head"))
    return (
        attended,
        query_grad.astype(jnp.bfloat16),
        value_grad.astype(jnp.bfloat16),
        totals[0] * scale,
        totals[1] * scale,
    )


def solution(mesh):
    placed = (
        P("ctx", "head", None),
        P("ctx", "head", None),
        P("ctx", "head", None),
        P(),
        P(),
        P("ctx"),
        P("ctx", "head", None),
    )
    return jax.shard_map(
        on_device,
        mesh=mesh,
        in_specs=placed,
        out_specs=(
            P("ctx", "head", None),
            P("ctx", "head", None),
            P("ctx", "head", None),
            P(),
            P(),
        ),
        check_vma=False,
    )
```

profile of v0, /device:TPU:0, one launch (start us, length us, event | category | flops | bytes accessed | tf_op | source)
XLA Modules:
  0.0 189.3 jit_solution(6467831528171327081)
XLA Ops:
  7.2 1.3 fusion.43
  8.5 1.1 copy.39
  10.3 1.3 fusion.39
  11.7 0.8 copy-done
  12.6 0.8 fusion.28
  17.5 23.2 %all-reduce.3 = (f32[8]{0:T(128)S(1)}, f32[8]{0:T(128)S(1)}) all-reduce(f32[8]{0:T(128)S(1)} %dynamic-update-slice, f32[8]{0:T(128)S(1)} %dynamic-update-slice.1), channel_id=1, replica_groups=mesh['ctx'=8,'head'=4] {'ctx'}, use_global_device_ids=true, to_apply=%add | all-reduce | flops 16 | bytes 128
  40.8 0.8 copy-done.2
  42.5 14.0 %all-gather.5.cloned.1.call-done = f32[16,128,128]{2,1,0:T(8,128)} async-done(((f32[2,128,128]{2,1,0:T(8,128)}), f32[16,128,128]{2,1,0:T(8,128)}) %all-gather.5.cloned.1.call-update) | async-done | bytes 1048592 | tf_op jit(solution)/shard_map/all_gather | solution.py:11
  56.4 24.9 %while.32 = (s32[]{:T(128)}, f32[2,128,128]{2,1,0:T(8,128)S(1)}, f32[]{:T(128)}, s32[]{:T(128)}, f32[8,2,128,128]{3,2,1,0:T(8,128)}, /*index=5*/f32[8]{0:T(128)S(1)}, s32[]{:T(128)}, f32[]{:T(128)}, s32[]{:T(128)}) while((s32[]{:T(128)}, f32[2,128,128]{2,1,0:T(8,128)S(1)}, f32[]{:T(128)}, s32[]{:T(128)}, ...), condition=%wide.region_1.2_spmd.clone, body=%wide.region_0.1_spmd.clone.sunk | while | flops 131082 | bytes 393401 | solution.py:23
  58.3 1.0 fusion.61
  61.9 1.0 fusion.61
  65.4 1.0 fusion.61
  69.0 1.0 fusion.61
  72.5 1.0 fusion.61
  76.1 1.0 fusion.61
  79.7 1.0 fusion.61
  82.8 0.9 fusion.26
  84.4 0.8 copy.62
  85.1 0.8 copy.61
  86.4 36.4 %all-gather.7.cloned.1.call-done = f32[16,128,128]{2,1,0:T(8,128)} async-done(((f32[2,128,128]{2,1,0:T(8,128)}), f32[16,128,128]{2,1,0:T(8,128)}) %all-gather.7.cloned.1.call-update) | async-done | bytes 1048592 | tf_op jit(solution)/shard_map/all_gather | solution.py:11
  122.7 1.3 rev.6
  124.0 18.4 %while.33 = (s32[]{:T(128)}, f32[2,128,128]{2,1,0:T(8,128)S(1)}, f32[]{:T(128)}, s32[]{:T(128)}, f32[8,2,128,128]{3,2,1,0:T(8,128)S(1)}, /*index=5*/f32[8]{0:T(128)S(1)}, s32[]{:T(128)}, f32[]{:T(128)}, s32[]{:T(128)}) while((s32[]{:T(128)}, f32[2,128,128]{2,1,0:T(8,128)S(1)}, f32[]{:T(128)}, s32[]{:T(128)}, ...), condition=%wide.region_5.6_spmd.clone, body=%wide.region_4.5_spmd.clone.sunk | while | flops 131082 | bytes 393401 | solution.py:23
  143.0 0.8 copy.63
  143.8 38.2 %all-reduce.2 = (f32[128]{0:T(128)S(1)}, f32[128]{0:T(128)S(1)}) all-reduce(f32[128]{0:T(128)S(1)} %fusion.17, f32[128]{0:T(128)S(1)} %get-tuple-element.281), channel_id=1, replica_groups=mesh['ctx'=8,'head'=4] {'ctx','head'}, use_global_device_ids=true, to_apply=%region_7.8 | all-reduce | flops 256 | bytes 2048 | tf_op jit(solution)/shard_map/psum | solution.py:105
  (65 shorter events, 16.8 us)
Async XLA Ops:
  7.2 49.3 %all-gather.5.cloned.1.call-start = ((), (), s32[]{:S(2)}) async-start(), calls=%async_computation | async-start | bytes 1179648 | tf_op jit(solution)/shard_map/all_gather | solution.py:11
  9.6 0.7 copy-start.3
  10.3 1.3 copy-start.5
  11.6 0.9 copy-start
  13.4 27.3 %copy-start.1 = (bf16[256,2,128]{2,1,0:T(2,128)(2,1)S(1)}, bf16[256,2,128]{2,1,0:T(2,128)(2,1)}, u32[]{:S(2)}) copy-start(bf16[256,2,128]{2,1,0:T(2,128)(2,1)} %param.11) | copy-start | bytes 393220
  13.4 109.3 %all-gather.7.cloned.1.call-start = ((), (), s32[]{:S(2)}) async-start(), calls=%async_computation.1 | async-start | bytes 1179648 | tf_op jit(solution)/shard_map/all_gather | solution.py:11
  14.8 0.7 copy-start.6
  40.7 0.9 copy-start.2
  81.8 0.7 copy-start.4
Sparse Core Ops, SparseCore 0:
  13.5 42.8 all-gather.4
  83.8 38.8 all-gather.6
where the time goes:
time: 190 us; the launch traced here: 189 us
  blocking collectives  61.4 us (32%)
  waiting for transfers between devices  50.4 us (27%)
  loops' own time  27.8 us (15%)
  local copies, waits for them, and re-layouts  20.2 us (11%)
  between operations  15.6 us (8%)
  other arithmetic  9.97 us (5%)
  matrix products  4 us (2%)
    all_gather x2, waiting for transfers between devices, entering(): pieces = jax.tree.map(lambda part: lax.all_gather(part, axis), value)  50.3 us
    psum x1, blocking collectives, on_device(): totals = lax.psum((thresh_term, gain_term), ('ctx', 'head'))  38.2 us
    another operation x2, loops' own time, entering(): return lax.fori_loop(0, count - 1, step, so_far)  27.8 us
    unnamed x1, blocking collectives  23.2 us
    unnamed x25, local copies, waits for them, and re-layouts  9.29 us
    dynamic_slice x14, local copies, waits for them, and re-layouts, step(): longer = join(so_far, jax.tree.map(lambda part: part[position], pieces))  8.2 us
    select_n x14, other arithmetic, step(): jnp.where(position < mine, new, old)  7.34 us
  transfers between devices with their start and end apart: 2, of which 2 were waited for; matrix products, arithmetic and copies ran while one was open for 3% of the time, Pallas kernels for 0%

commit v1 on v0

v1 whole, which is shorter than its diff:
```python
import functools
import math

import jax
import jax.numpy as jnp
from jax import lax
from jax.experimental import pallas as pl
from jax.experimental.pallas import tpu as pltpu
from jax.sharding import PartitionSpec as P

BF16 = jnp.bfloat16
F32 = jnp.float32
MARK_ROWS = 8
VMEM_LIMIT = 48 * 1024 * 1024


def row_iota(shape):
    return lax.broadcasted_iota(jnp.int32, shape, 0)


def col_iota(shape):
    return lax.broadcasted_iota(jnp.int32, shape, 1)


def dot_nn(a, b):
    return lax.dot_general(a, b, (((1,), (0,)), ((), ())), preferred_element_type=F32)


def dot_nt(a, b):
    return lax.dot_general(a, b, (((1,), (1,)), ((), ())), preferred_element_type=F32)


def dot_tn(a, b):
    return lax.dot_general(a, b, (((0,), (0,)), ((), ())), preferred_element_type=F32)


def head_docs(ids):
    return ids[:, :1]


def tail_docs(ids):
    return ids[:, ids.shape[1] - 1 :]


def first_rows(ids, heads, rows):
    count = jnp.sum((ids == head_docs(ids)).astype(jnp.int32), axis=1, keepdims=True)
    return row_iota((rows, 1)) < heads * count


def last_rows(ids, heads, rows):
    count = jnp.sum((ids != tail_docs(ids)).astype(jnp.int32), axis=1, keepdims=True)
    return row_iota((rows, 1)) >= heads * count


def split_heads(x, keep, heads):
    head = lax.rem(row_iota((x.shape[0], 1)), heads)
    return jnp.concatenate(
        [jnp.where(keep & (head == h), x, jnp.zeros_like(x)) for h in range(heads)], axis=1
    )


def pick_heads(parts, keep):
    heads = len(parts)
    head = lax.rem(row_iota((parts[0].shape[0], 1)), heads)
    out = jnp.zeros_like(parts[0])
    for h in range(heads):
        out = jnp.where(keep & (head == h), parts[h], out)
    return out


def put_message(out_ref, state, mark):
    count = state.shape[0]
    out_ref[:count, :] = state
    out_ref[count:, :] = jnp.broadcast_to(mark.astype(F32), (MARK_ROWS, out_ref.shape[1]))


def take_messages(refs, mark):
    total = None
    for ref in refs:
        count = ref.shape[0] - MARK_ROWS
        same = (ref[count : count + 1, :] == mark.astype(F32)).astype(F32)
        part = ref[:count, :] * same
        total = part if total is None else total + part
    return total.astype(BF16)


def tail_kernel(heads, spikes_ref, values_ref, threshold_ref, ids_ref, tail_ref):
    ids = ids_ref[...]
    rows = values_ref.shape[0]
    keys = (spikes_ref[...].astype(F32) * threshold_ref[...]).astype(BF16)
    spread = split_heads(keys, last_rows(ids, heads, rows), heads)
    put_message(tail_ref, dot_tn(spread, values_ref[...]), tail_docs(ids))


def inside_kernel(
    heads, queries_ref, spikes_ref, values_ref, threshold_ref, ids_ref,
    base_ref, scores_ref, mask_ref, keys_ref,
):
    rows = queries_ref.shape[0]
    tokens = ids_ref.shape[1]
    queries = queries_ref[...]
    keys = (spikes_ref[...].astype(F32) * threshold_ref[...]).astype(BF16)
    keys_ref[...] = keys
    ids = ids_ref[...].astype(F32)
    apart = row_iota((rows, tokens)) - heads * col_iota((rows, tokens))
    down = jnp.sum(
        jnp.where((apart >= 0) & (apart < heads), ids, 0.0), axis=1, keepdims=True
    )
    r = row_iota((rows, rows))
    c = col_iota((rows, rows))
    across = jnp.sum(jnp.where(r == c, down, 0.0), axis=0, keepdims=True)
    allowed = (c <= r) & (down == across) & (lax.rem(r - c, heads) == 0)
    scores = jnp.where(allowed, dot_nt(queries, keys), 0.0).astype(BF16)
    scores_ref[...] = scores
    mask_ref[...] = allowed.astype(BF16)
    base_ref[...] = queries.astype(F32) + dot_nn(scores, values_ref[...])


def middle_kernel(
    heads, hops, queries_ref, values_ref, cotangent_ref, base_ref, mask_ref, keys_ref,
    threshold_ref, gain_ref, ids_ref, *refs,
):
    received = refs[:hops]
    attended_ref, query_grad_ref, gnorm_ref, back_ref, partial_ref = refs[hops:]
    rows, width = queries_ref.shape
    ids = ids_ref[...]
    queries = queries_ref[...]
    first = first_rows(ids, heads, rows)
    carried = take_messages(received, head_docs(ids))
    states = [carried[h * width : (h + 1) * width, :] for h in range(heads)]
    mixed = base_ref[...] + pick_heads([dot_nn(queries, s) for s in states], first)
    ratio = lax.rsqrt(jnp.mean(mixed * mixed, axis=1, keepdims=True) + 1e-06)
    normed = mixed * ratio
    gain = gain_ref[...]
    attended_ref[...] = (normed * gain).astype(BF16)
    cotangent = cotangent_ref[...].astype(F32)
    upstream = cotangent * gain
    inner = jnp.mean(normed * upstream, axis=1, keepdims=True)
    gnorm = (ratio * upstream - normed * ratio * inner).astype(BF16)
    gnorm_ref[...] = gnorm
    put_message(back_ref, dot_tn(split_heads(queries, first, heads), gnorm), head_docs(ids))
    dscores = (dot_nt(gnorm, values_ref[...]) * mask_ref[...].astype(F32)).astype(BF16)
    mixing = dot_nn(dscores, keys_ref[...])
    mixing = mixing + pick_heads([dot_nt(gnorm, s) for s in states], first)
    query_grad_ref[...] = (gnorm.astype(F32) + mixing).astype(BF16)
    threshold_part = (
        jnp.sum(queries.astype(F32) * mixing, axis=0, keepdims=True) / threshold_ref[...]
    )
    gain_part = jnp.sum(cotangent * normed, axis=0, keepdims=True)
    both = jnp.concatenate([threshold_part, gain_part], axis=0)
    partial_ref[...] = jnp.broadcast_to(both[None], partial_ref.shape)


def last_kernel(
    heads, hops, scale, gnorm_ref, scores_ref, keys_ref, ids_ref, parts_ref, *refs
):
    received = refs[:hops]
    value_grad_ref, threshold_grad_ref, gain_grad_ref = refs[hops:]
    rows, width = gnorm_ref.shape
    ids = ids_ref[...]
    returned = take_messages(received, tail_docs(ids))
    states = [returned[h * width : (h + 1) * width, :] for h in range(heads)]
    keys = keys_ref[...]
    across = pick_heads([dot_nn(keys, s) for s in states], last_rows(ids, heads, rows))
    value_grad_ref[...] = (dot_tn(scores_ref[...], gnorm_ref[...]) + across).astype(BF16)
    parts = parts_ref[...]
    even = lax.rem(row_iota(parts.shape), 2) == 0
    threshold_grad_ref[...] = jnp.sum(jnp.where(even, parts, 0.0), axis=0, keepdims=True) * scale
    gain_grad_ref[...] = jnp.sum(jnp.where(even, 0.0, parts), axis=0, keepdims=True) * scale


def call(kernel, name, out, *args):
    size = sum(a.size * a.dtype.itemsize for a in (*args, *out))
    return pl.pallas_call(
        kernel,
        name=name,
        out_shape=out,
        in_specs=[pl.BlockSpec(memory_space=pltpu.VMEM)] * len(args),
        out_specs=[pl.BlockSpec(memory_space=pltpu.VMEM)] * len(out),
        compiler_params=pltpu.CompilerParams(vmem_limit_bytes=VMEM_LIMIT),
        cost_estimate=pl.CostEstimate(flops=10**8, bytes_accessed=size, transcendentals=0),
    )(*args)


def shifted(x, by):
    count = lax.axis_size("ctx")
    pairs = [(i, i + by) for i in range(count) if 0 <= i + by < count]
    return lax.ppermute(x, "ctx", pairs)


def neighbours(message, reach, sign):
    if reach <= 3:
        return [shifted(message, sign * by) for by in range(1, reach + 1)]
    rows = message.shape[0] - MARK_ROWS
    state, marks = message[:rows], message[rows:]
    window = 1
    while window < reach:
        other = shifted(jnp.concatenate([state, marks]), sign * window)
        same = (other[rows:][:1] == marks[:1]).astype(F32)
        state = state + same * other[:rows]
        window = 2 * window
    return [shifted(jnp.concatenate([state, marks]), sign)]


def on_device(queries, spikes, values, threshold, norm_gain, document_ids, cotangent):
    length, heads, width = queries.shape
    rows = length * heads
    blocks = lax.axis_size("ctx")
    devices = blocks * lax.axis_size("head")
    reach = -(-(length * blocks // 4 - 1) // length)
    flat = lambda x: x.reshape(rows, width)
    q, s, v, ct = flat(queries), flat(spikes), flat(values), flat(cotangent)
    thr, gain, ids = threshold[None], norm_gain[None], document_ids[None]
    like = jax.ShapeDtypeStruct
    message = like((heads * width + MARK_ROWS, width), F32)

    (tail,) = call(functools.partial(tail_kernel, heads), "tail", [message], s, v, thr, ids)
    ahead = neighbours(tail, reach, 1)
    base, scores, mask, keys = call(
        functools.partial(inside_kernel, heads),
        "inside",
        [like((rows, width), F32), like((rows, rows), BF16), like((rows, rows), BF16),
         like((rows, width), BF16)],
        q, s, v, thr, ids,
    )
    attended, query_grad, gnorm, back, partial = call(
        functools.partial(middle_kernel, heads, len(ahead)),
        "middle",
        [like((rows, width), BF16), like((rows, width), BF16), like((rows, width), BF16),
         message, like((devices, 2, width), F32)],
        q, v, ct, base, mask, keys, thr, gain, ids, *ahead,
    )
    behind = neighbours(back, reach, -1)
    parts = lax.all_to_all(partial, ("ctx", "head"), 0, 0)
    scale = 1.0 / math.sqrt(rows * devices)
    value_grad, threshold_grad, gain_grad = call(
        functools.partial(last_kernel, heads, len(behind), scale),
        "last",
        [like((rows, width), BF16), like((1, width), F32), like((1, width), F32)],
        gnorm, scores, keys, ids, parts.reshape(2 * devices, width), *behind,
    )
    whole = lambda x: x.reshape(length, heads, width)
    return (
        whole(attended),
        whole(query_grad),
        whole(value_grad),
        threshold_grad[0],
        gain_grad[0],
    )


def solution(mesh):
    block = P("ctx", "head", None)
    return jax.shard_map(
        on_device,
        mesh=mesh,
        in_specs=(block, block, block, P(), P(), P("ctx"), block),
        out_specs=(block, block, block, P(), P()),
        check_vma=False,
    )
```

time: 190 us -> 38.1 us (0.20)
  waiting for transfers between devices: 50.4 us -> 1.82 us
  blocking collectives: 61.4 us -> 17 us
  loops' own time: 27.8 us -> 0 us
  local copies, waits for them, and re-layouts: 20.2 us -> 3.19 us
  between operations: 15.6 us -> 0.74 us
  starting transfers between devices: 0.08 us -> 10.9 us
  other arithmetic: 9.97 us -> 0 us
  Pallas kernels: 0 us -> 4.18 us
  matrix products: 4 us -> 0 us
    all_gather x2 -> x0, waiting for transfers between devices: 50.3 us -> none  [entering(): pieces = jax.tree.map(lambda part: lax.all_gather(part, axis), value)]
    psum x1 -> x0, blocking collectives: 38.2 us -> none  [on_device(): totals = lax.psum((thresh_term, gain_term), ('ctx', 'head'))]
    another operation x2 -> x0, loops' own time: 27.8 us -> none  [entering(): return lax.fori_loop(0, count - 1, step, so_far)]
    unnamed x1 -> x0, blocking collectives: 23.2 us -> none
    all_to_all x0 -> x1, blocking collectives: none -> 17 us  [on_device(): parts = lax.all_to_all(partial, ('ctx', 'head'), 0, 0)]
    ppermute x0 -> x4, starting transfers between devices: none -> 10.9 us  [shifted(): return lax.ppermute(x, 'ctx', pairs)]
    dynamic_slice x14 -> x0, local copies, waits for them, and re-layouts: 8.2 us -> none  [step(): longer = join(so_far, jax.tree.map(lambda part: part[position], pieces))]
    select_n x14 -> x0, other arithmetic: 7.34 us -> none  [step(): jnp.where(position < mine, new, old)]
  transfers between devices with their start and end apart: 2 -> 4, of which waited for: 2 -> 1; matrix products, arithmetic and copies ran while one was open for 3% -> 0% of each run, Pallas kernels for 0% -> 2%
where the time goes in v1:
time: 38.1 us; the launch traced here: 37.9 us
  blocking collectives  17 us (45%)
  starting transfers between devices  10.9 us (29%)
  Pallas kernels  4.18 us (11%)
  local copies, waits for them, and re-layouts  3.19 us (8%)
  waiting for transfers between devices  1.82 us (5%)
  between operations  0.74 us (2%)
    all_to_all x1, blocking collectives, on_device(): parts = lax.all_to_all(partial, ('ctx', 'head'), 0, 0)  17 us
    ppermute x4, starting transfers between devices, shifted(): return lax.ppermute(x, 'ctx', pairs)  10.9 us
    pallas_call x4, Pallas kernels, call(): pl.pallas_call(kernel, name=name, out_shape=out, in_specs=[pl.BlockSpec(m...  4.18 us
    unnamed x18, local copies, waits for them, and re-layouts  3.19 us
    ppermute x4, waiting for transfers between devices, shifted(): return lax.ppermute(x, 'ctx', pairs)  1.82 us
  transfers between devices with their start and end apart: 4, of which 1 were waited for; matrix products, arithmetic and copies ran while one was open for 0% of the time, Pallas kernels for 2%

profile of v1, /device:TPU:0, one launch (start us, length us, event | category | flops | bytes accessed | tf_op | source)
XLA Modules:
  0.0 37.9 jit_solution(2811399882521126221)
XLA Ops:
  0.6 0.0 copy-start.6
  0.6 0.0 copy-start.7
  0.7 0.7 %copy-done.6 = s32[256]{0:T(256)S(1)} copy-done((s32[256]{0:T(256)S(1)}, s32[256]{0:T(256)}, u32[]{:S(2)}) %copy-start.6) | copy-done | bytes 1048
  1.3 0.9 %copy-done = bf16[256,2,128]{2,1,0:T(2,128)(2,1)S(1)} copy-done((bf16[256,2,128]{2,1,0:T(2,128)(2,1)S(1)}, bf16[256,2,128]{2,1,0:T(2,128)(2,1)}, u32[]{:S(2)}) %copy-start) | copy-done | bytes 131096
  2.2 0.9 %copy-done.2 = s32[256,2,128]{2,1,0:T(2,128)S(1)} copy-done((s32[256,2,128]{2,1,0:T(2,128)S(1)}, s32[256,2,128]{2,1,0:T(2,128)}, u32[]{:S(2)}) %copy-start.2) | copy-done | bytes 262168
  3.2 0.5 %tail.1 = f32[264,128]{1,0:T(8,128)S(1)} custom-call(s32[512,128]{1,0:T(8,128)S(1)} %bitcast.16, bf16[512,128]{1,0:T(8,128)(2,1)S(1)} %bitcast.13, f32[1,128]{1,0:T(1,128)S(1)} %bitcast.26, s32[1,256]{1,0:T(1,128)S(1)} %bitcast.22), custom_call_target="tpu_custom_call" | custom-call | flops 100000000 | bytes 529920 | tf_op jit(solution)/shard_map/tail/pallas_call | solution.py:174
  3.7 4.9 %collective-permute-start.1 = (f32[264,128]{1,0:T(8,128)S(1)}, f32[264,128]{1,0:T(8,128)S(1)}, u32[]{:S(2)}, u32[]{:S(2)}) collective-permute-start(f32[264,128]{1,0:T(8,128)S(1)} %tail.1), channel_id=1, source_target_pairs={{0,8},{4,12},{8,16},{12,20},{16,24},{20,28},{1,9},{5,13},{9,17},{1... | collective-permute-start | bytes 405512 | tf_op jit(solution)/shard_map/ppermute | solution.py:188
  8.6 3.4 %collective-permute-start = (f32[264,128]{1,0:T(8,128)S(1)}, f32[264,128]{1,0:T(8,128)S(1)}, u32[]{:S(2)}, u32[]{:S(2)}) collective-permute-start(f32[264,128]{1,0:T(8,128)S(1)} %tail.1), channel_id=1, source_target_pairs={{0,4},{4,8},{8,12},{12,16},{16,20},{20,24},{24,28},{1,5},{5,9},{9,... | collective-permute-start | bytes 405512 | tf_op jit(solution)/shard_map/ppermute | solution.py:188
  12.0 0.0 copy-done.1
  12.0 0.0 copy-done.3
  12.0 0.0 copy-done.4
  12.0 0.0 copy-start.5
  12.1 0.7 %inside.1 = (f32[512,128]{1,0:T(8,128)S(1)}, bf16[512,512]{1,0:T(8,128)(2,1)S(1)}, bf16[512,512]{1,0:T(8,128)(2,1)S(1)}, bf16[512,128]{1,0:T(8,128)(2,1)S(1)}) custom-call(bf16[512,128]{1,0:T(8,128)(2,1)S(1)} %bitcast.18, s32[512,128]{1,0:T(8,128)S(1)} %bitcast.17, bf16[512,128]{1,0:T(8,128)(2,1)S(1)} %bitcast.14, f32[1,128]{1,0:T(1,128)S(1)} %bitcast.27, ...), custom_call_target="tpu_custom_call" | custom-call | flops 100000000 | bytes 1967616 | tf_op jit(solution)/shard_map/inside/pallas_call | solution.py:174
  12.7 0.0 collective-permute-done.1.refs_1_
  12.7 1.8 %collective-permute-done.refs_0_ = f32[264,128]{1,0:T(8,128)S(1)} collective-permute-done((f32[264,128]{1,0:T(8,128)S(1)}, f32[264,128]{1,0:T(8,128)S(1)}, u32[]{:S(2)}, u32[]{:S(2)}) %collective-permute-start) | collective-permute-done | bytes 135200 | tf_op jit(solution)/shard_map/ppermute | solution.py:188
  14.6 0.0 copy-done.5
  14.6 0.7 %copy-done.8 = f32[128]{0:T(128)S(1)} copy-done((f32[128]{0:T(128)S(1)}, f32[128]{0:T(128)}, u32[]{:S(2)}) %copy-start.8) | copy-done | bytes 536
  15.2 1.8 %middle.1 = (bf16[512,128]{1,0:T(8,128)(2,1)}, bf16[512,128]{1,0:T(8,128)(2,1)}, bf16[512,128]{1,0:T(8,128)(2,1)S(1)}, f32[264,128]{1,0:T(8,128)S(1)}, f32[32,2,128]{2,1,0:T(2,128)S(1)}) custom-call(bf16[512,128]{1,0:T(8,128)(2,1)S(1)} %bitcast.19, bf16[512,128]{1,0:T(8,128)(2,1)S(1)} %bitcast.15, bf16[512,128]{1,0:T(8,128)(2,1)S(1)} %bitcast.20, ...), custom_call_target="tpu_custom_call" | custom-call | flops 100000000 | bytes 2144256 | tf_op jit(solution)/shard_map/middle/pallas_call | solution.py:174
  17.0 1.3 %collective-permute-start.3 = (f32[264,128]{1,0:T(8,128)S(1)}, f32[264,128]{1,0:T(8,128)S(1)}, u32[]{:S(2)}, u32[]{:S(2)}) collective-permute-start(f32[264,128]{1,0:T(8,128)S(1)} %get-tuple-element.25), channel_id=1, source_target_pairs={{8,0},{12,4},{16,8},{20,12},{24,16},{28,20},{9,1},{13,5},{17,9},{2... | collective-permute-start | bytes 405512 | tf_op jit(solution)/shard_map/ppermute | solution.py:188
  18.3 1.3 %collective-permute-start.2 = (f32[264,128]{1,0:T(8,128)S(1)}, f32[264,128]{1,0:T(8,128)S(1)}, u32[]{:S(2)}, u32[]{:S(2)}) collective-permute-start(f32[264,128]{1,0:T(8,128)S(1)} %get-tuple-element.25), channel_id=1, source_target_pairs={{4,0},{8,4},{12,8},{16,12},{20,16},{24,20},{28,24},{5,1},{9,5},{13... | collective-permute-start | bytes 405512 | tf_op jit(solution)/shard_map/ppermute | solution.py:188
  19.6 17.0 %all_to_all.5 = f32[32,2,128]{2,1,0:T(2,128)S(1)} all-to-all(f32[32,2,128]{2,1,0:T(2,128)S(1)} %get-tuple-element.24), channel_id=1, replica_groups=mesh['ctx'=8,'head'=4] {'ctx','head'}, dimensions={0} | all-to-all | bytes 65536 | tf_op jit(solution)/shard_map/all_to_all | solution.py:234
  36.6 0.0 collective-permute-done.3.refs_1_
  36.6 0.0 collective-permute-done.2.refs_0_
  36.6 1.2 %last.1 = (bf16[512,128]{1,0:T(8,128)(2,1)}, f32[1,128]{1,0:T(1,128)}, f32[1,128]{1,0:T(1,128)}) custom-call(bf16[512,128]{1,0:T(8,128)(2,1)S(1)} %get-tuple-element.22.gnorm_ref, bf16[512,512]{1,0:T(8,128)(2,1)S(1)} %get-tuple-element.23.scores_ref, bf16[512,128]{1,0:T(8,128)(2,1)S(1)} %get-tuple-element.19.keys_ref, s32[1,256]{1,0:T(1,128)S(1)} %bitcast.25, ...), custom_call_target="tpu_custom_call" | custom-call | flops 100000000 | bytes 1222656 | tf_op jit(solution)/shard_map/last/pallas_call | solution.py:174
  (7 shorter events, 0.0 us)
Async XLA Ops:
  0.6 0.7 %copy-start.6 = (s32[256]{0:T(256)S(1)}, s32[256]{0:T(256)}, u32[]{:S(2)}) copy-start(s32[256]{0:T(256)} %param.12) | copy-start | bytes 3076
  0.6 0.7 %copy-start.7 = (f32[128]{0:T(128)S(1)}, f32[128]{0:T(128)}, u32[]{:S(2)}) copy-start(f32[128]{0:T(128)} %param.10) | copy-start | bytes 1540
  1.3 0.9 %copy-start = (bf16[256,2,128]{2,1,0:T(2,128)(2,1)S(1)}, bf16[256,2,128]{2,1,0:T(2,128)(2,1)}, u32[]{:S(2)}) copy-start(bf16[256,2,128]{2,1,0:T(2,128)(2,1)} %param.9) | copy-start | bytes 393220
  2.2 0.9 %copy-start.2 = (s32[256,2,128]{2,1,0:T(2,128)S(1)}, s32[256,2,128]{2,1,0:T(2,128)}, u32[]{:S(2)}) copy-start(s32[256,2,128]{2,1,0:T(2,128)} %param.8) | copy-start | bytes 786436
  3.2 8.8 %copy-start.1 = (bf16[256,2,128]{2,1,0:T(2,128)(2,1)S(1)}, bf16[256,2,128]{2,1,0:T(2,128)(2,1)}, u32[]{:S(2)}) copy-start(bf16[256,2,128]{2,1,0:T(2,128)(2,1)} %param.9) | copy-start | bytes 393220
  3.2 8.9 %copy-start.3 = (s32[256,2,128]{2,1,0:T(2,128)S(1)}, s32[256,2,128]{2,1,0:T(2,128)}, u32[]{:S(2)}) copy-start(s32[256,2,128]{2,1,0:T(2,128)} %param.8) | copy-start | bytes 786436
  3.2 8.9 %copy-start.4 = (bf16[256,2,128]{2,1,0:T(2,128)(2,1)S(1)}, bf16[256,2,128]{2,1,0:T(2,128)(2,1)}, u32[]{:S(2)}) copy-start(bf16[256,2,128]{2,1,0:T(2,128)(2,1)} %param.7) | copy-start | bytes 393220
  3.7 9.1 %collective-permute-start.1 = (f32[264,128]{1,0:T(8,128)S(1)}, f32[264,128]{1,0:T(8,128)S(1)}, u32[]{:S(2)}, u32[]{:S(2)}) collective-permute-start(f32[264,128]{1,0:T(8,128)S(1)} %tail.1), channel_id=1, source_target_pairs={{0,8},{4,12},{8,16},{12,20},{16,24},{20,28},{1,9},{5,13},{9,17},{1... | collective-permute-start | bytes 405512 | tf_op jit(solution)/shard_map/ppermute | solution.py:188
  8.6 5.9 %collective-permute-start = (f32[264,128]{1,0:T(8,128)S(1)}, f32[264,128]{1,0:T(8,128)S(1)}, u32[]{:S(2)}, u32[]{:S(2)}) collective-permute-start(f32[264,128]{1,0:T(8,128)S(1)} %tail.1), channel_id=1, source_target_pairs={{0,4},{4,8},{8,12},{12,16},{16,20},{20,24},{24,28},{1,5},{5,9},{9,... | collective-permute-start | bytes 405512 | tf_op jit(solution)/shard_map/ppermute | solution.py:188
  12.0 2.5 %copy-start.5 = (bf16[256,2,128]{2,1,0:T(2,128)(2,1)S(1)}, bf16[256,2,128]{2,1,0:T(2,128)(2,1)}, u32[]{:S(2)}) copy-start(bf16[256,2,128]{2,1,0:T(2,128)(2,1)} %param.13) | copy-start | bytes 393220
  14.6 0.7 %copy-start.8 = (f32[128]{0:T(128)S(1)}, f32[128]{0:T(128)}, u32[]{:S(2)}) copy-start(f32[128]{0:T(128)} %param.11) | copy-start | bytes 1540
  17.0 19.6 %collective-permute-start.3 = (f32[264,128]{1,0:T(8,128)S(1)}, f32[264,128]{1,0:T(8,128)S(1)}, u32[]{:S(2)}, u32[]{:S(2)}) collective-permute-start(f32[264,128]{1,0:T(8,128)S(1)} %get-tuple-element.25), channel_id=1, source_target_pairs={{8,0},{12,4},{16,8},{20,12},{24,16},{28,20},{9,1},{13,5},{17,9},{2... | collective-permute-start | bytes 405512 | tf_op jit(solution)/shard_map/ppermute | solution.py:188
  18.3 18.3 %collective-permute-start.2 = (f32[264,128]{1,0:T(8,128)S(1)}, f32[264,128]{1,0:T(8,128)S(1)}, u32[]{:S(2)}, u32[]{:S(2)}) collective-permute-start(f32[264,128]{1,0:T(8,128)S(1)} %get-tuple-element.25), channel_id=1, source_target_pairs={{4,0},{8,4},{12,8},{16,12},{20,16},{24,20},{28,24},{5,1},{9,5},{13... | collective-permute-start | bytes 405512 | tf_op jit(solution)/shard_map/ppermute | solution.py:188

commit v2 on v1

--- a/solution.py
+++ b/solution.py
@@ -184,7 +184,7 @@
 
 def shifted(x, by):
     count = lax.axis_size("ctx")
-    pairs = [(i, i + by) for i in range(count) if 0 <= i + by < count]
+    pairs = [(i, (i + by) % count) for i in range(count)]
     return lax.ppermute(x, "ctx", pairs)
 
 

time: 38.1 us -> 32.2 us (0.85)
  blocking collectives: 17 us -> 10.4 us
  waiting for transfers between devices: 1.82 us -> 7.26 us
  starting transfers between devices: 10.9 us -> 6.31 us
    all_to_all x1, blocking collectives: 17 us -> 10.4 us  [on_device(): parts = lax.all_to_all(partial, ('ctx', 'head'), 0, 0)]
    ppermute x4, waiting for transfers between devices: 1.82 us -> 7.26 us  [shifted(): return lax.ppermute(x, 'ctx', pairs)]
    ppermute x4, starting transfers between devices: 10.9 us -> 6.31 us  [shifted(): return lax.ppermute(x, 'ctx', pairs)]
  transfers between devices with their start and end apart: 4 -> 4, of which waited for: 1 -> 2; matrix products, arithmetic and copies ran while one was open for 0% -> 0% of each run, Pallas kernels for 2% -> 2%
where the time goes in v2:
time: 32.2 us; the launch traced here: 32 us
  blocking collectives  10.4 us (32%)
  waiting for transfers between devices  7.26 us (23%)
  starting transfers between devices  6.31 us (20%)
  Pallas kernels  4.17 us (13%)
  local copies, waits for them, and re-layouts  3.19 us (10%)
  between operations  0.68 us (2%)
    all_to_all x1, blocking collectives, on_device(): parts = lax.all_to_all(partial, ('ctx', 'head'), 0, 0)  10.4 us
    ppermute x4, waiting for transfers between devices, shifted(): return lax.ppermute(x, 'ctx', pairs)  7.26 us
    ppermute x4, starting transfers between devices, shifted(): return lax.ppermute(x, 'ctx', pairs)  6.31 us
    pallas_call x4, Pallas kernels, call(): pl.pallas_call(kernel, name=name, out_shape=out, in_specs=[pl.BlockSpec(m...  4.17 us
    unnamed x18, local copies, waits for them, and re-layouts  3.19 us
  transfers between devices with their start and end apart: 4, of which 2 were waited for; matrix products, arithmetic and copies ran while one was open for 0% of the time, Pallas kernels for 2%

profile of v2, /device:TPU:0, one launch (start us, length us, event | category | flops | bytes accessed | tf_op | source)
XLA Modules:
  0.0 32.0 jit_solution(6735495523955442503)
XLA Ops:
  0.6 0.0 copy-start.6
  0.6 0.0 copy-start.7
  0.7 0.7 %copy-done.6 = s32[256]{0:T(256)S(1)} copy-done((s32[256]{0:T(256)S(1)}, s32[256]{0:T(256)}, u32[]{:S(2)}) %copy-start.6) | copy-done | bytes 1048
  1.3 0.0 copy-done.7
  1.3 0.9 %copy-done = bf16[256,2,128]{2,1,0:T(2,128)(2,1)S(1)} copy-done((bf16[256,2,128]{2,1,0:T(2,128)(2,1)S(1)}, bf16[256,2,128]{2,1,0:T(2,128)(2,1)}, u32[]{:S(2)}) %copy-start) | copy-done | bytes 131096
  2.2 0.9 %copy-done.2 = s32[256,2,128]{2,1,0:T(2,128)S(1)} copy-done((s32[256,2,128]{2,1,0:T(2,128)S(1)}, s32[256,2,128]{2,1,0:T(2,128)}, u32[]{:S(2)}) %copy-start.2) | copy-done | bytes 262168
  3.2 0.5 %tail.1 = f32[264,128]{1,0:T(8,128)S(1)} custom-call(s32[512,128]{1,0:T(8,128)S(1)} %bitcast.16, bf16[512,128]{1,0:T(8,128)(2,1)S(1)} %bitcast.13, f32[1,128]{1,0:T(1,128)S(1)} %bitcast.26, s32[1,256]{1,0:T(1,128)S(1)} %bitcast.22), custom_call_target="tpu_custom_call" | custom-call | flops 100000000 | bytes 529920 | tf_op jit(solution)/shard_map/tail/pallas_call | solution.py:174
  3.7 3.1 %collective-permute-start.1 = (f32[264,128]{1,0:T(8,128)S(1)}, f32[264,128]{1,0:T(8,128)S(1)}, u32[]{:S(2)}, u32[]{:S(2)}) collective-permute-start(f32[264,128]{1,0:T(8,128)S(1)} %tail.1), channel_id=1, source_target_pairs={{0,8},{4,12},{8,16},{12,20},{16,24},{20,28},{24,0},{28,4},{1,9},{5... | collective-permute-start | bytes 405512 | tf_op jit(solution)/shard_map/ppermute | solution.py:188
  6.7 1.5 %collective-permute-start = (f32[264,128]{1,0:T(8,128)S(1)}, f32[264,128]{1,0:T(8,128)S(1)}, u32[]{:S(2)}, u32[]{:S(2)}) collective-permute-start(f32[264,128]{1,0:T(8,128)S(1)} %tail.1), channel_id=1, source_target_pairs={{0,4},{4,8},{8,12},{12,16},{16,20},{20,24},{24,28},{28,0},{1,5},{5... | collective-permute-start | bytes 405512 | tf_op jit(solution)/shard_map/ppermute | solution.py:188
  8.2 0.0 copy-done.1
  8.2 0.0 copy-done.3
  8.2 0.0 copy-done.4
  8.2 0.7 %inside.1 = (f32[512,128]{1,0:T(8,128)S(1)}, bf16[512,512]{1,0:T(8,128)(2,1)S(1)}, bf16[512,512]{1,0:T(8,128)(2,1)S(1)}, bf16[512,128]{1,0:T(8,128)(2,1)S(1)}) custom-call(bf16[512,128]{1,0:T(8,128)(2,1)S(1)} %bitcast.18, s32[512,128]{1,0:T(8,128)S(1)} %bitcast.17, bf16[512,128]{1,0:T(8,128)(2,1)S(1)} %bitcast.14, f32[1,128]{1,0:T(1,128)S(1)} %bitcast.27, ...), custom_call_target="tpu_custom_call" | custom-call | flops 100000000 | bytes 1967616 | tf_op jit(solution)/shard_map/inside/pallas_call | solution.py:174
  8.9 3.4 %collective-permute-done.1.refs_1_ = f32[264,128]{1,0:T(8,128)S(1)} collective-permute-done((f32[264,128]{1,0:T(8,128)S(1)}, f32[264,128]{1,0:T(8,128)S(1)}, u32[]{:S(2)}, u32[]{:S(2)}) %collective-permute-start.1) | collective-permute-done | bytes 135200 | tf_op jit(solution)/shard_map/ppermute | solution.py:188
  12.3 3.8 %collective-permute-done.refs_0_ = f32[264,128]{1,0:T(8,128)S(1)} collective-permute-done((f32[264,128]{1,0:T(8,128)S(1)}, f32[264,128]{1,0:T(8,128)S(1)}, u32[]{:S(2)}, u32[]{:S(2)}) %collective-permute-start) | collective-permute-done | bytes 135200 | tf_op jit(solution)/shard_map/ppermute | solution.py:188
  16.2 0.0 copy-done.5
  16.2 0.7 %copy-done.8 = f32[128]{0:T(128)S(1)} copy-done((f32[128]{0:T(128)S(1)}, f32[128]{0:T(128)}, u32[]{:S(2)}) %copy-start.8) | copy-done | bytes 536
  16.8 1.8 %middle.1 = (bf16[512,128]{1,0:T(8,128)(2,1)}, bf16[512,128]{1,0:T(8,128)(2,1)}, bf16[512,128]{1,0:T(8,128)(2,1)S(1)}, f32[264,128]{1,0:T(8,128)S(1)}, f32[32,2,128]{2,1,0:T(2,128)S(1)}) custom-call(bf16[512,128]{1,0:T(8,128)(2,1)S(1)} %bitcast.19, bf16[512,128]{1,0:T(8,128)(2,1)S(1)} %bitcast.15, bf16[512,128]{1,0:T(8,128)(2,1)S(1)} %bitcast.20, ...), custom_call_target="tpu_custom_call" | custom-call | flops 100000000 | bytes 2144256 | tf_op jit(solution)/shard_map/middle/pallas_call | solution.py:174
  18.6 1.7 %collective-permute-start.3 = (f32[264,128]{1,0:T(8,128)S(1)}, f32[264,128]{1,0:T(8,128)S(1)}, u32[]{:S(2)}, u32[]{:S(2)}) collective-permute-start(f32[264,128]{1,0:T(8,128)S(1)} %get-tuple-element.25), channel_id=1, source_target_pairs={{0,24},{4,28},{8,0},{12,4},{16,8},{20,12},{24,16},{28,20},{1,25},{... | collective-permute-start | bytes 405512 | tf_op jit(solution)/shard_map/ppermute | solution.py:188
  20.4 0.0 collective-permute-start.2
  20.4 10.4 %all_to_all.5 = f32[32,2,128]{2,1,0:T(2,128)S(1)} all-to-all(f32[32,2,128]{2,1,0:T(2,128)S(1)} %get-tuple-element.24), channel_id=1, replica_groups=mesh['ctx'=8,'head'=4] {'ctx','head'}, dimensions={0} | all-to-all | bytes 65536 | tf_op jit(solution)/shard_map/all_to_all | solution.py:234
  30.8 0.0 collective-permute-done.3.refs_1_
  30.8 0.0 collective-permute-done.2.refs_0_
  30.8 1.2 %last.1 = (bf16[512,128]{1,0:T(8,128)(2,1)}, f32[1,128]{1,0:T(1,128)}, f32[1,128]{1,0:T(1,128)}) custom-call(bf16[512,128]{1,0:T(8,128)(2,1)S(1)} %get-tuple-element.22.gnorm_ref, bf16[512,512]{1,0:T(8,128)(2,1)S(1)} %get-tuple-element.23.scores_ref, bf16[512,128]{1,0:T(8,128)(2,1)S(1)} %get-tuple-element.19.keys_ref, s32[1,256]{1,0:T(1,128)S(1)} %bitcast.25, ...), custom_call_target="tpu_custom_call" | custom-call | flops 100000000 | bytes 1222656 | tf_op jit(solution)/shard_map/last/pallas_call | solution.py:174
  (7 shorter events, 0.0 us)
Async XLA Ops:
  0.6 0.7 %copy-start.6 = (s32[256]{0:T(256)S(1)}, s32[256]{0:T(256)}, u32[]{:S(2)}) copy-start(s32[256]{0:T(256)} %param.12) | copy-start | bytes 3076
  0.6 0.7 %copy-start.7 = (f32[128]{0:T(128)S(1)}, f32[128]{0:T(128)}, u32[]{:S(2)}) copy-start(f32[128]{0:T(128)} %param.10) | copy-start | bytes 1540
  1.3 0.9 %copy-start = (bf16[256,2,128]{2,1,0:T(2,128)(2,1)S(1)}, bf16[256,2,128]{2,1,0:T(2,128)(2,1)}, u32[]{:S(2)}) copy-start(bf16[256,2,128]{2,1,0:T(2,128)(2,1)} %param.9) | copy-start | bytes 393220
  2.2 0.9 %copy-start.2 = (s32[256,2,128]{2,1,0:T(2,128)S(1)}, s32[256,2,128]{2,1,0:T(2,128)}, u32[]{:S(2)}) copy-start(s32[256,2,128]{2,1,0:T(2,128)} %param.8) | copy-start | bytes 786436
  3.2 5.1 %copy-start.1 = (bf16[256,2,128]{2,1,0:T(2,128)(2,1)S(1)}, bf16[256,2,128]{2,1,0:T(2,128)(2,1)}, u32[]{:S(2)}) copy-start(bf16[256,2,128]{2,1,0:T(2,128)(2,1)} %param.9) | copy-start | bytes 393220
  3.2 5.1 %copy-start.3 = (s32[256,2,128]{2,1,0:T(2,128)S(1)}, s32[256,2,128]{2,1,0:T(2,128)}, u32[]{:S(2)}) copy-start(s32[256,2,128]{2,1,0:T(2,128)} %param.8) | copy-start | bytes 786436
  3.2 5.1 %copy-start.4 = (bf16[256,2,128]{2,1,0:T(2,128)(2,1)S(1)}, bf16[256,2,128]{2,1,0:T(2,128)(2,1)}, u32[]{:S(2)}) copy-start(bf16[256,2,128]{2,1,0:T(2,128)(2,1)} %param.7) | copy-start | bytes 393220
  3.7 8.7 %collective-permute-start.1 = (f32[264,128]{1,0:T(8,128)S(1)}, f32[264,128]{1,0:T(8,128)S(1)}, u32[]{:S(2)}, u32[]{:S(2)}) collective-permute-start(f32[264,128]{1,0:T(8,128)S(1)} %tail.1), channel_id=1, source_target_pairs={{0,8},{4,12},{8,16},{12,20},{16,24},{20,28},{24,0},{28,4},{1,9},{5... | collective-permute-start | bytes 405512 | tf_op jit(solution)/shard_map/ppermute | solution.py:188
  6.7 9.4 %collective-permute-start = (f32[264,128]{1,0:T(8,128)S(1)}, f32[264,128]{1,0:T(8,128)S(1)}, u32[]{:S(2)}, u32[]{:S(2)}) collective-permute-start(f32[264,128]{1,0:T(8,128)S(1)} %tail.1), channel_id=1, source_target_pairs={{0,4},{4,8},{8,12},{12,16},{16,20},{20,24},{24,28},{28,0},{1,5},{5... | collective-permute-start | bytes 405512 | tf_op jit(solution)/shard_map/ppermute | solution.py:188
  8.2 7.9 %copy-start.5 = (bf16[256,2,128]{2,1,0:T(2,128)(2,1)S(1)}, bf16[256,2,128]{2,1,0:T(2,128)(2,1)}, u32[]{:S(2)}) copy-start(bf16[256,2,128]{2,1,0:T(2,128)(2,1)} %param.13) | copy-start | bytes 393220
  16.2 0.7 %copy-start.8 = (f32[128]{0:T(128)S(1)}, f32[128]{0:T(128)}, u32[]{:S(2)}) copy-start(f32[128]{0:T(128)} %param.11) | copy-start | bytes 1540
  18.6 12.1 %collective-permute-start.3 = (f32[264,128]{1,0:T(8,128)S(1)}, f32[264,128]{1,0:T(8,128)S(1)}, u32[]{:S(2)}, u32[]{:S(2)}) collective-permute-start(f32[264,128]{1,0:T(8,128)S(1)} %get-tuple-element.25), channel_id=1, source_target_pairs={{0,24},{4,28},{8,0},{12,4},{16,8},{20,12},{24,16},{28,20},{1,25},{... | collective-permute-start | bytes 405512 | tf_op jit(solution)/shard_map/ppermute | solution.py:188
  20.4 10.4 %collective-permute-start.2 = (f32[264,128]{1,0:T(8,128)S(1)}, f32[264,128]{1,0:T(8,128)S(1)}, u32[]{:S(2)}, u32[]{:S(2)}) collective-permute-start(f32[264,128]{1,0:T(8,128)S(1)} %get-tuple-element.25), channel_id=1, source_target_pairs={{0,28},{4,0},{8,4},{12,8},{16,12},{20,16},{24,20},{28,24},{1,29},{... | collective-permute-start | bytes 405512 | tf_op jit(solution)/shard_map/ppermute | solution.py:188

commit v3 on v2

--- a/solution.py
+++ b/solution.py
@@ -52,19 +52,19 @@
     return row_iota((rows, 1)) >= heads * count
 
 
-def split_heads(x, keep, heads):
+def spread_heads(x, keep, heads):
     head = lax.rem(row_iota((x.shape[0], 1)), heads)
     return jnp.concatenate(
         [jnp.where(keep & (head == h), x, jnp.zeros_like(x)) for h in range(heads)], axis=1
     )
 
 
-def pick_heads(parts, keep):
-    heads = len(parts)
-    head = lax.rem(row_iota((parts[0].shape[0], 1)), heads)
-    out = jnp.zeros_like(parts[0])
+def pick_heads(x, keep, heads):
+    width = x.shape[1] // heads
+    head = lax.rem(row_iota((x.shape[0], 1)), heads)
+    out = jnp.zeros((x.shape[0], width), x.dtype)
     for h in range(heads):
-        out = jnp.where(keep & (head == h), parts[h], out)
+        out = jnp.where(keep & (head == h), x[:, h * width : (h + 1) * width], out)
     return out
 
 
@@ -84,23 +84,31 @@
     return total.astype(BF16)
 
 
-def tail_kernel(heads, spikes_ref, values_ref, threshold_ref, ids_ref, tail_ref):
+def pattern_kernel(heads, causal_ref, start_ref):
+    r, c = row_iota(causal_ref.shape), col_iota(causal_ref.shape)
+    causal_ref[...] = ((c <= r) & (lax.rem(r - c, heads) == 0)).astype(BF16)
+    start_ref[...] = jnp.zeros_like(start_ref)
+
+
+def tail_kernel(
+    heads, spikes_ref, values_ref, threshold_ref, gain_ref, ids_ref, start_ref, tail_ref, keys_ref,
+    gain_out_ref,
+):
+    gain_out_ref[...] = gain_ref[...]
     ids = ids_ref[...]
     rows = values_ref.shape[0]
     keys = (spikes_ref[...].astype(F32) * threshold_ref[...]).astype(BF16)
-    spread = split_heads(keys, last_rows(ids, heads, rows), heads)
-    put_message(tail_ref, dot_tn(spread, values_ref[...]), tail_docs(ids))
+    keys_ref[...] = keys
+    spread = spread_heads(values_ref[...], last_rows(ids, heads, rows), heads)
+    put_message(tail_ref, dot_tn(keys, spread), tail_docs(ids))
 
 
 def inside_kernel(
-    heads, queries_ref, spikes_ref, values_ref, threshold_ref, ids_ref,
-    base_ref, scores_ref, mask_ref, keys_ref,
+    heads, queries_ref, keys_ref, values_ref, ids_ref, causal_ref, base_ref, scores_ref, mask_ref
 ):
     rows = queries_ref.shape[0]
     tokens = ids_ref.shape[1]
     queries = queries_ref[...]
-    keys = (spikes_ref[...].astype(F32) * threshold_ref[...]).astype(BF16)
-    keys_ref[...] = keys
     ids = ids_ref[...].astype(F32)
     apart = row_iota((rows, tokens)) - heads * col_iota((rows, tokens))
     down = jnp.sum(
@@ -109,10 +117,10 @@
     r = row_iota((rows, rows))
     c = col_iota((rows, rows))
     across = jnp.sum(jnp.where(r == c, down, 0.0), axis=0, keepdims=True)
-    allowed = (c <= r) & (down == across) & (lax.rem(r - c, heads) == 0)
-    scores = jnp.where(allowed, dot_nt(queries, keys), 0.0).astype(BF16)
+    allowed = jnp.where(down == across, causal_ref[...].astype(F32), 0.0).astype(BF16)
+    scores = dot_nt(queries, keys_ref[...]).astype(BF16) * allowed
     scores_ref[...] = scores
-    mask_ref[...] = allowed.astype(BF16)
+    mask_ref[...] = allowed
     base_ref[...] = queries.astype(F32) + dot_nn(scores, values_ref[...])
 
 
@@ -122,13 +130,12 @@
 ):
     received = refs[:hops]
     attended_ref, query_grad_ref, gnorm_ref, back_ref, partial_ref = refs[hops:]
-    rows, width = queries_ref.shape
+    rows = queries_ref.shape[0]
     ids = ids_ref[...]
     queries = queries_ref[...]
     first = first_rows(ids, heads, rows)
     carried = take_messages(received, head_docs(ids))
-    states = [carried[h * width : (h + 1) * width, :] for h in range(heads)]
-    mixed = base_ref[...] + pick_heads([dot_nn(queries, s) for s in states], first)
+    mixed = base_ref[...] + pick_heads(dot_nn(queries, carried), first, heads)
     ratio = lax.rsqrt(jnp.mean(mixed * mixed, axis=1, keepdims=True) + 1e-06)
     normed = mixed * ratio
     gain = gain_ref[...]
@@ -138,10 +145,10 @@
     inner = jnp.mean(normed * upstream, axis=1, keepdims=True)
     gnorm = (ratio * upstream - normed * ratio * inner).astype(BF16)
     gnorm_ref[...] = gnorm
-    put_message(back_ref, dot_tn(split_heads(queries, first, heads), gnorm), head_docs(ids))
-    dscores = (dot_nt(gnorm, values_ref[...]) * mask_ref[...].astype(F32)).astype(BF16)
-    mixing = dot_nn(dscores, keys_ref[...])
-    mixing = mixing + pick_heads([dot_nt(gnorm, s) for s in states], first)
+    spread = spread_heads(gnorm, first, heads)
+    put_message(back_ref, dot_tn(queries, spread), head_docs(ids))
+    dscores = dot_nt(gnorm, values_ref[...]).astype(BF16) * mask_ref[...]
+    mixing = dot_nn(dscores, keys_ref[...]) + dot_nt(spread, carried)
     query_grad_ref[...] = (gnorm.astype(F32) + mixing).astype(BF16)
     threshold_part = (
         jnp.sum(queries.astype(F32) * mixing, axis=0, keepdims=True) / threshold_ref[...]
@@ -152,33 +159,52 @@
 
 
 def last_kernel(
-    heads, hops, scale, gnorm_ref, scores_ref, keys_ref, ids_ref, parts_ref, *refs
+    heads, hops, scale, gnorm_ref, scores_ref, keys_ref, ids_ref, parts_ref,
+    attended_ref, query_grad_ref, *refs,
 ):
     received = refs[:hops]
-    value_grad_ref, threshold_grad_ref, gain_grad_ref = refs[hops:]
-    rows, width = gnorm_ref.shape
-    ids = ids_ref[...]
-    returned = take_messages(received, tail_docs(ids))
-    states = [returned[h * width : (h + 1) * width, :] for h in range(heads)]
-    keys = keys_ref[...]
-    across = pick_heads([dot_nn(keys, s) for s in states], last_rows(ids, heads, rows))
-    value_grad_ref[...] = (dot_tn(scores_ref[...], gnorm_ref[...]) + across).astype(BF16)
+    attended_hbm, query_grad_hbm, value_grad_hbm, threshold_hbm, gain_hbm = refs[hops : hops + 5]
+    value_grad_ref, threshold_ref, gain_ref, sems = refs[hops + 5 :]
+    copies = [
+        pltpu.make_async_copy(attended_ref, attended_hbm, sems.at[0]),
+        pltpu.make_async_copy(query_grad_ref, query_grad_hbm, sems.at[1]),
+        pltpu.make_async_copy(value_grad_ref, value_grad_hbm, sems.at[2]),
+        pltpu.make_async_copy(threshold_ref, threshold_hbm, sems.at[3]),
+        pltpu.make_async_copy(gain_ref, gain_hbm, sems.at[4]),
+    ]
+    copies[0].start()
+    copies[1].start()
     parts = parts_ref[...]
     even = lax.rem(row_iota(parts.shape), 2) == 0
-    threshold_grad_ref[...] = jnp.sum(jnp.where(even, parts, 0.0), axis=0, keepdims=True) * scale
-    gain_grad_ref[...] = jnp.sum(jnp.where(even, 0.0, parts), axis=0, keepdims=True) * scale
-
-
-def call(kernel, name, out, *args):
+    threshold_ref[...] = jnp.sum(jnp.where(even, parts, 0.0), axis=0, keepdims=True) * scale
+    copies[3].start()
+    gain_ref[...] = jnp.sum(jnp.where(even, 0.0, parts), axis=0, keepdims=True) * scale
+    copies[4].start()
+    ids = ids_ref[...]
+    rows = gnorm_ref.shape[0]
+    returned = take_messages(received, tail_docs(ids))
+    across = pick_heads(dot_nn(keys_ref[...], returned), last_rows(ids, heads, rows), heads)
+    value_grad_ref[...] = (dot_tn(scores_ref[...], gnorm_ref[...]) + across).astype(BF16)
+    copies[2].start()
+    for copy in copies:
+        copy.wait()
+
+
+VMEM = pl.BlockSpec(memory_space=pltpu.VMEM)
+HBM = pl.BlockSpec(memory_space=pltpu.HBM)
+
+
+def call(kernel, name, out, args, in_space=VMEM, out_spaces=None, scratch=(), flops=10**8):
     size = sum(a.size * a.dtype.itemsize for a in (*args, *out))
     return pl.pallas_call(
         kernel,
         name=name,
         out_shape=out,
-        in_specs=[pl.BlockSpec(memory_space=pltpu.VMEM)] * len(args),
-        out_specs=[pl.BlockSpec(memory_space=pltpu.VMEM)] * len(out),
+        in_specs=[in_space] * len(args),
+        out_specs=out_spaces or [VMEM] * len(out),
+        scratch_shapes=list(scratch),
         compiler_params=pltpu.CompilerParams(vmem_limit_bytes=VMEM_LIMIT),
-        cost_estimate=pl.CostEstimate(flops=10**8, bytes_accessed=size, transcendentals=0),
+        cost_estimate=pl.CostEstimate(flops=flops, bytes_accessed=size, transcendentals=0),
     )(*args)
 
 
@@ -212,32 +238,48 @@
     q, s, v, ct = flat(queries), flat(spikes), flat(values), flat(cotangent)
     thr, gain, ids = threshold[None], norm_gain[None], document_ids[None]
     like = jax.ShapeDtypeStruct
-    message = like((heads * width + MARK_ROWS, width), F32)
-
-    (tail,) = call(functools.partial(tail_kernel, heads), "tail", [message], s, v, thr, ids)
+    message = like((width + MARK_ROWS, heads * width), F32)
+    flat_bf = like((rows, width), BF16)
+    row_f = like((1, width), F32)
+
+    causal, start = call(
+        functools.partial(pattern_kernel, heads),
+        "pattern",
+        [like((rows, rows), BF16), like((8, 128), F32)],
+        (),
+        flops=4 * 10**9,
+    )
+    tail, keys, gain = call(
+        functools.partial(tail_kernel, heads),
+        "tail",
+        [message, flat_bf, row_f],
+        (s, v, thr, gain, ids, start),
+    )
     ahead = neighbours(tail, reach, 1)
-    base, scores, mask, keys = call(
+    base, scores, mask = call(
         functools.partial(inside_kernel, heads),
         "inside",
-        [like((rows, width), F32), like((rows, rows), BF16), like((rows, rows), BF16),
-         like((rows, width), BF16)],
-        q, s, v, thr, ids,
+        [like((rows, width), F32), like((rows, rows), BF16), like((rows, rows), BF16)],
+        (q, keys, v, ids, causal),
     )
     attended, query_grad, gnorm, back, partial = call(
         functools.partial(middle_kernel, heads, len(ahead)),
         "middle",
-        [like((rows, width), BF16), like((rows, width), BF16), like((rows, width), BF16),
-         message, like((devices, 2, width), F32)],
-        q, v, ct, base, mask, keys, thr, gain, ids, *ahead,
+        [flat_bf, flat_bf, flat_bf, message, like((devices, 2, width), F32)],
+        (q, v, ct, base, mask, keys, thr, gain, ids, *ahead),
     )
     behind = neighbours(back, reach, -1)
     parts = lax.all_to_all(partial, ("ctx", "head"), 0, 0)
     scale = 1.0 / math.sqrt(rows * devices)
-    value_grad, threshold_grad, gain_grad = call(
+    attended, query_grad, value_grad, threshold_grad, gain_grad = call(
         functools.partial(last_kernel, heads, len(behind), scale),
         "last",
-        [like((rows, width), BF16), like((1, width), F32), like((1, width), F32)],
-        gnorm, scores, keys, ids, parts.reshape(2 * devices, width), *behind,
+        [flat_bf, flat_bf, flat_bf, row_f, row_f],
+        (gnorm, scores, keys, ids, parts.reshape(2 * devices, width), attended, query_grad,
+         *behind),
+        out_spaces=[HBM] * 5,
+        scratch=[pltpu.VMEM((rows, width), BF16), pltpu.VMEM((1, width), F32),
+                 pltpu.VMEM((1, width), F32), pltpu.SemaphoreType.DMA((5,))],
     )
     whole = lambda x: x.reshape(length, heads, width)
     return (

time: 32.2 us -> 29.5 us (0.916)
  local copies, waits for them, and re-layouts: 3.19 us -> 0.82 us
  Pallas kernels: 4.17 us -> 3.48 us
  waiting for transfers between devices: 7.26 us -> 7.6 us
    unnamed x18 -> x14, local copies, waits for them, and re-layouts: 3.19 us -> 0.82 us
    pallas_call x4 -> x5, Pallas kernels: 4.17 us -> 3.48 us  [call(): pl.pallas_call(kernel, name=name, out_shape=out, in_specs=[in_space] * le...]
    ppermute x4, waiting for transfers between devices: 7.26 us -> 7.6 us  [shifted(): return lax.ppermute(x, 'ctx', pairs)]
where the time goes in v3:
time: 29.5 us; the launch traced here: 29.4 us
  blocking collectives  10.4 us (35%)
  waiting for transfers between devices  7.6 us (26%)
  starting transfers between devices  6.36 us (22%)
  Pallas kernels  3.48 us (12%)
  local copies, waits for them, and re-layouts  0.82 us (3%)
  between operations  0.71 us (2%)
    all_to_all x1, blocking collectives, on_device(): parts = lax.all_to_all(partial, ('ctx', 'head'), 0, 0)  10.4 us
    ppermute x4, waiting for transfers between devices, shifted(): return lax.ppermute(x, 'ctx', pairs)  7.6 us
    ppermute x4, starting transfers between devices, shifted(): return lax.ppermute(x, 'ctx', pairs)  6.36 us
    pallas_call x5, Pallas kernels, call(): pl.pallas_call(kernel, name=name, out_shape=out, in_specs=[in_space] * le...  3.48 us
    unnamed x14, local copies, waits for them, and re-layouts  0.82 us
  transfers between devices with their start and end apart: 4, of which 2 were waited for; matrix products, arithmetic and copies ran while one was open for 0% of the time, Pallas kernels for 2%

profile of v3, /device:TPU:0, one launch (start us, length us, event | category | flops | bytes accessed | tf_op | source)
XLA Modules:
  0.0 29.4 jit_solution(8205862327249780317)
XLA Ops:
  0.6 0.0 copy-start
  0.6 0.0 copy-start.2
  0.7 0.0 copy-start.6
  0.7 0.2 pattern.1
  0.8 0.0 copy-start.4
  0.9 0.0 copy-start.5
  0.9 0.7 %copy-done = bf16[256,2,128]{2,1,0:T(2,128)(2,1)S(1)} copy-done((bf16[256,2,128]{2,1,0:T(2,128)(2,1)S(1)}, bf16[256,2,128]{2,1,0:T(2,128)(2,1)}, u32[]{:S(2)}) %copy-start) | copy-done | bytes 131096
  1.5 0.1 copy-done.2
  1.7 0.0 copy-done.6
  1.7 0.0 copy-done.5
  1.7 0.4 %tail.1 = (f32[136,256]{1,0:T(8,128)S(1)}, bf16[512,128]{1,0:T(8,128)(2,1)S(1)}, f32[1,128]{1,0:T(1,128)S(1)}) custom-call(s32[512,128]{1,0:T(8,128)S(1)} %bitcast.18, bf16[512,128]{1,0:T(8,128)(2,1)S(1)} %bitcast.13, f32[1,128]{1,0:T(1,128)S(1)} %bitcast.25, f32[1,128]{1,0:T(1,128)S(1)} %bitcast.27, s32[1,256]{1,0:T(1,128)S(1)} %bitcast.21, ...), custom_call_target="tpu_custom_call" | custom-call | flops 100000000 | bytes 670208 | tf_op jit(solution)/shard_map/tail/pallas_call | solution.py:199
  2.1 3.1 %collective-permute-start.1 = (f32[136,256]{1,0:T(8,128)S(1)}, f32[136,256]{1,0:T(8,128)S(1)}, u32[]{:S(2)}, u32[]{:S(2)}) collective-permute-start(f32[136,256]{1,0:T(8,128)S(1)} %get-tuple-element.29), channel_id=1, source_target_pairs={{0,8},{4,12},{8,16},{12,20},{16,24},{20,28},{24,0},{28,4},{1,9},{5... | collective-permute-start | bytes 417800 | tf_op jit(solution)/shard_map/ppermute | solution.py:214
  5.1 1.5 %collective-permute-start = (f32[136,256]{1,0:T(8,128)S(1)}, f32[136,256]{1,0:T(8,128)S(1)}, u32[]{:S(2)}, u32[]{:S(2)}) collective-permute-start(f32[136,256]{1,0:T(8,128)S(1)} %get-tuple-element.29), channel_id=1, source_target_pairs={{0,4},{4,8},{8,12},{12,16},{16,20},{20,24},{24,28},{28,0},{1,5},{5... | collective-permute-start | bytes 417800 | tf_op jit(solution)/shard_map/ppermute | solution.py:214
  6.6 0.0 copy-done.1
  6.6 0.5 %inside.1 = (f32[512,128]{1,0:T(8,128)S(1)}, bf16[512,512]{1,0:T(8,128)(2,1)S(1)}, bf16[512,512]{1,0:T(8,128)(2,1)S(1)}) custom-call(bf16[512,128]{1,0:T(8,128)(2,1)S(1)} %bitcast.16, bf16[512,128]{1,0:T(8,128)(2,1)S(1)} %get-tuple-element.24.keys_ref, bf16[512,128]{1,0:T(8,128)(2,1)S(1)} %bitcast.14, s32[1,256]{1,0:T(1,128)S(1)} %bitcast.22, ...), custom_call_target="tpu_custom_call" | custom-call | flops 100000000 | bytes 2229248 | tf_op jit(solution)/shard_map/inside/pallas_call | solution.py:199
  7.2 3.7 %collective-permute-done.1.refs_1_ = f32[136,256]{1,0:T(8,128)S(1)} collective-permute-done((f32[136,256]{1,0:T(8,128)S(1)}, f32[136,256]{1,0:T(8,128)S(1)}, u32[]{:S(2)}, u32[]{:S(2)}) %collective-permute-start.1) | collective-permute-done | bytes 139296 | tf_op jit(solution)/shard_map/ppermute | solution.py:214
  10.8 3.9 %collective-permute-done.refs_0_ = f32[136,256]{1,0:T(8,128)S(1)} collective-permute-done((f32[136,256]{1,0:T(8,128)S(1)}, f32[136,256]{1,0:T(8,128)S(1)}, u32[]{:S(2)}, u32[]{:S(2)}) %collective-permute-start) | collective-permute-done | bytes 139296 | tf_op jit(solution)/shard_map/ppermute | solution.py:214
  14.8 1.1 %middle.1 = (bf16[512,128]{1,0:T(8,128)(2,1)S(1)}, bf16[512,128]{1,0:T(8,128)(2,1)S(1)}, bf16[512,128]{1,0:T(8,128)(2,1)S(1)}, f32[136,256]{1,0:T(8,128)S(1)}, f32[32,2,128]{2,1,0:T(2,128)S(1)}) custom-call(bf16[512,128]{1,0:T(8,128)(2,1)S(1)} %bitcast.17, bf16[512,128]{1,0:T(8,128)(2,1)S(1)} %bitcast.15, bf16[512,128]{1,0:T(8,128)(2,1)S(1)} %bitcast.19, ...), custom_call_target="tpu_custom_call" | custom-call | flops 100000000 | bytes 2156544 | tf_op jit(solution)/shard_map/middle/pallas_call | solution.py:199
  15.9 1.8 %collective-permute-start.3 = (f32[136,256]{1,0:T(8,128)S(1)}, f32[136,256]{1,0:T(8,128)S(1)}, u32[]{:S(2)}, u32[]{:S(2)}) collective-permute-start(f32[136,256]{1,0:T(8,128)S(1)} %get-tuple-element.35), channel_id=1, source_target_pairs={{0,24},{4,28},{8,0},{12,4},{16,8},{20,12},{24,16},{28,20},{1,25},{... | collective-permute-start | bytes 417800 | tf_op jit(solution)/shard_map/ppermute | solution.py:214
  17.7 0.0 collective-permute-start.2
  17.7 10.4 %all_to_all.5 = f32[32,2,128]{2,1,0:T(2,128)S(1)} all-to-all(f32[32,2,128]{2,1,0:T(2,128)S(1)} %get-tuple-element.32), channel_id=1, replica_groups=mesh['ctx'=8,'head'=4] {'ctx','head'}, dimensions={0} | all-to-all | bytes 65536 | tf_op jit(solution)/shard_map/all_to_all | solution.py:272
  28.1 0.0 collective-permute-done.3.refs_1_
  28.1 0.0 collective-permute-done.2.refs_0_
  28.1 1.2 %last.1 = (bf16[512,128]{1,0:T(8,128)(2,1)}, bf16[512,128]{1,0:T(8,128)(2,1)}, bf16[512,128]{1,0:T(8,128)(2,1)}, f32[1,128]{1,0:T(1,128)}, f32[1,128]{1,0:T(1,128)}) custom-call(bf16[512,128]{1,0:T(8,128)(2,1)S(1)} %get-tuple-element.30.gnorm_ref, bf16[512,512]{1,0:T(8,128)(2,1)S(1)} %get-tuple-element.31.scores_ref, ...), custom_call_target="tpu_custom_call" | custom-call | flops 100000000 | bytes 1755136 | tf_op jit(solution)/shard_map/last/pallas_call | solution.py:199
  (4 shorter events, 0.0 us)
Async XLA Ops:
  0.6 0.9 %copy-start = (bf16[256,2,128]{2,1,0:T(2,128)(2,1)S(1)}, bf16[256,2,128]{2,1,0:T(2,128)(2,1)}, u32[]{:S(2)}) copy-start(bf16[256,2,128]{2,1,0:T(2,128)(2,1)} %param.9) | copy-start | bytes 393220
  0.6 1.0 %copy-start.2 = (s32[256,2,128]{2,1,0:T(2,128)S(1)}, s32[256,2,128]{2,1,0:T(2,128)}, u32[]{:S(2)}) copy-start(s32[256,2,128]{2,1,0:T(2,128)} %param.8) | copy-start | bytes 786436
  0.7 1.0 %copy-start.6 = (f32[128]{0:T(128)S(1)}, f32[128]{0:T(128)}, u32[]{:S(2)}) copy-start(f32[128]{0:T(128)} %param.11) | copy-start | bytes 1540
  0.8 0.8 %copy-start.4 = (s32[256]{0:T(256)S(1)}, s32[256]{0:T(256)}, u32[]{:S(2)}) copy-start(s32[256]{0:T(256)} %param.12) | copy-start | bytes 3076
  0.9 0.8 %copy-start.5 = (f32[128]{0:T(128)S(1)}, f32[128]{0:T(128)}, u32[]{:S(2)}) copy-start(f32[128]{0:T(128)} %param.10) | copy-start | bytes 1540
  1.7 5.0 %copy-start.1 = (bf16[256,2,128]{2,1,0:T(2,128)(2,1)S(1)}, bf16[256,2,128]{2,1,0:T(2,128)(2,1)}, u32[]{:S(2)}) copy-start(bf16[256,2,128]{2,1,0:T(2,128)(2,1)} %param.7) | copy-start | bytes 393220
  2.1 8.8 %collective-permute-start.1 = (f32[136,256]{1,0:T(8,128)S(1)}, f32[136,256]{1,0:T(8,128)S(1)}, u32[]{:S(2)}, u32[]{:S(2)}) collective-permute-start(f32[136,256]{1,0:T(8,128)S(1)} %get-tuple-element.29), channel_id=1, source_target_pairs={{0,8},{4,12},{8,16},{12,20},{16,24},{20,28},{24,0},{28,4},{1,9},{5... | collective-permute-start | bytes 417800 | tf_op jit(solution)/shard_map/ppermute | solution.py:214
  5.1 9.6 %collective-permute-start = (f32[136,256]{1,0:T(8,128)S(1)}, f32[136,256]{1,0:T(8,128)S(1)}, u32[]{:S(2)}, u32[]{:S(2)}) collective-permute-start(f32[136,256]{1,0:T(8,128)S(1)} %get-tuple-element.29), channel_id=1, source_target_pairs={{0,4},{4,8},{8,12},{12,16},{16,20},{20,24},{24,28},{28,0},{1,5},{5... | collective-permute-start | bytes 417800 | tf_op jit(solution)/shard_map/ppermute | solution.py:214
  6.6 8.1 %copy-start.3 = (bf16[256,2,128]{2,1,0:T(2,128)(2,1)S(1)}, bf16[256,2,128]{2,1,0:T(2,128)(2,1)}, u32[]{:S(2)}) copy-start(bf16[256,2,128]{2,1,0:T(2,128)(2,1)} %param.13) | copy-start | bytes 393220
  15.9 12.2 %collective-permute-start.3 = (f32[136,256]{1,0:T(8,128)S(1)}, f32[136,256]{1,0:T(8,128)S(1)}, u32[]{:S(2)}, u32[]{:S(2)}) collective-permute-start(f32[136,256]{1,0:T(8,128)S(1)} %get-tuple-element.35), channel_id=1, source_target_pairs={{0,24},{4,28},{8,0},{12,4},{16,8},{20,12},{24,16},{28,20},{1,25},{... | collective-permute-start | bytes 417800 | tf_op jit(solution)/shard_map/ppermute | solution.py:214
  17.7 10.4 %collective-permute-start.2 = (f32[136,256]{1,0:T(8,128)S(1)}, f32[136,256]{1,0:T(8,128)S(1)}, u32[]{:S(2)}, u32[]{:S(2)}) collective-permute-start(f32[136,256]{1,0:T(8,128)S(1)} %get-tuple-element.35), channel_id=1, source_target_pairs={{0,28},{4,0},{8,4},{12,8},{16,12},{20,16},{24,20},{28,24},{1,29},{... | collective-permute-start | bytes 417800 | tf_op jit(solution)/shard_map/ppermute | solution.py:214

commit v4 on v3

v4 whole, which is shorter than its diff:
```python
import functools
import math

import jax
import jax.numpy as jnp
from jax import lax
from jax.experimental import pallas as pl
from jax.experimental.pallas import tpu as pltpu
from jax.sharding import PartitionSpec as P

BF16 = jnp.bfloat16
F32 = jnp.float32
MARK_ROWS = 8
VMEM_LIMIT = 48 * 1024 * 1024


def row_iota(shape):
    return lax.broadcasted_iota(jnp.int32, shape, 0)


def col_iota(shape):
    return lax.broadcasted_iota(jnp.int32, shape, 1)


def dot_nn(a, b):
    return lax.dot_general(a, b, (((1,), (0,)), ((), ())), preferred_element_type=F32)


def dot_nt(a, b):
    return lax.dot_general(a, b, (((1,), (1,)), ((), ())), preferred_element_type=F32)


def dot_tn(a, b):
    return lax.dot_general(a, b, (((0,), (0,)), ((), ())), preferred_element_type=F32)


def spread_heads(x, own_ref):
    return jnp.concatenate([x * own_ref[h] for h in range(own_ref.shape[0])], axis=1)


def pick_heads(x, keep, own_ref):
    heads, _, width = own_ref.shape
    out = x[:, :width]
    for h in range(1, heads):
        out = jnp.where(own_ref[h] > 0, x[:, h * width : (h + 1) * width], out)
    return out * keep


def put_message(out_ref, state, mark_ref):
    count = state.shape[0]
    out_ref[:count, :] = state
    out_ref[count:, :] = mark_ref[...]


def take_messages(refs, mark_ref):
    total = None
    for ref in refs:
        count = ref.shape[0] - MARK_ROWS
        same = (ref[count : count + 1, :] == mark_ref[:1, :]).astype(F32)
        part = ref[:count, :] * same
        total = part if total is None else total + part
    return total.astype(BF16)


def pattern_kernel(heads, own_ref):
    head = lax.rem(row_iota(own_ref.shape[1:]), heads)
    for h in range(heads):
        own_ref[h] = (head == h).astype(BF16)


def marks_kernel(
    heads, ids_ref, threshold_ref, first_ref, last_ref, head_mark_ref, tail_mark_ref, threshold_out_ref
):
    threshold_out_ref[...] = threshold_ref[...]
    ids = ids_ref[...]
    head, tail = ids[:, :1], ids[:, ids.shape[1] - 1 :]
    in_first = jnp.sum((ids == head).astype(jnp.int32), axis=1, keepdims=True)
    before_last = jnp.sum((ids != tail).astype(jnp.int32), axis=1, keepdims=True)
    row = row_iota(first_ref.shape)
    first_ref[...] = (row < heads * in_first).astype(F32)
    last_ref[...] = (row >= heads * before_last).astype(F32)
    head_mark_ref[...] = jnp.broadcast_to(head.astype(F32), head_mark_ref.shape)
    tail_mark_ref[...] = jnp.broadcast_to(tail.astype(F32), tail_mark_ref.shape)


def tail_kernel(
    heads, spikes_ref, values_ref, threshold_ref, last_ref, tail_mark_ref, own_ref, tail_ref, keys_ref
):
    keys = spikes_ref[...].astype(F32) * threshold_ref[...]
    keys_ref[...] = keys.astype(BF16)
    kept = (keys * last_ref[...]).astype(BF16)
    put_message(tail_ref, dot_tn(kept, spread_heads(values_ref[...], own_ref)), tail_mark_ref)


def inside_kernel(
    heads, queries_ref, keys_ref, values_ref, cotangent_ref, gain_ref, ids_ref,
    base_ref, scores_t_ref, mask_ref, queries_t_ref, values_t_ref, own_ref, upstream_ref, gain_out_ref,
):
    rows = queries_ref.shape[0]
    tokens = ids_ref.shape[1]
    queries = queries_ref[...]
    ids = ids_ref[...].astype(F32)
    apart = row_iota((rows, tokens)) - heads * col_iota((rows, tokens))
    down = jnp.sum(
        jnp.where((apart >= 0) & (apart < heads), ids, 0.0), axis=1, keepdims=True
    )
    r = row_iota((rows, rows))
    c = col_iota((rows, rows))
    across = jnp.sum(jnp.where(r == c, down, 0.0), axis=0, keepdims=True)
    together = (down == across) & (lax.rem(r - c, heads) == 0)
    allowed = (together & (c <= r)).astype(F32).astype(BF16)
    allowed_t = (together & (r <= c)).astype(F32).astype(BF16)
    keys = keys_ref[...]
    scores = dot_nt(queries, keys).astype(BF16) * allowed
    scores_t_ref[...] = dot_nt(keys, queries).astype(BF16) * allowed_t
    mask_ref[...] = allowed
    queries_t_ref[...] = queries.T
    values_t_ref[...] = values_ref[...].T
    head = lax.rem(row_iota(own_ref.shape[1:]), heads)
    for h in range(heads):
        own_ref[h] = (head == h).astype(F32)
    gain_out_ref[...] = gain_ref[...]
    upstream_ref[...] = cotangent_ref[...].astype(F32) * gain_ref[...]
    base_ref[...] = queries.astype(F32) + dot_nn(scores, values_ref[...])


def middle_kernel(
    heads, hops, queries_ref, queries_t_ref, values_t_ref, cotangent_ref, upstream_ref, base_ref, mask_ref, keys_ref,
    threshold_ref, gain_ref, first_ref, head_mark_ref, own_ref, own_f_ref, *refs,
):
    received = refs[:hops]
    attended_ref, query_grad_ref, gnorm_ref, back_ref, partial_ref = refs[hops:]
    rows, width = queries_ref.shape
    carried = take_messages(received, head_mark_ref)
    gain = gain_ref[...]
    first = first_ref[...]
    queries = queries_ref[...]
    mixed = base_ref[...] + pick_heads(dot_nn(queries, carried), first, own_f_ref)
    cotangent = cotangent_ref[...].astype(F32)
    upstream = upstream_ref[...]
    square = jnp.mean(mixed * mixed, axis=1, keepdims=True)
    inner = jnp.mean(mixed * upstream, axis=1, keepdims=True)
    ratio = lax.rsqrt(square + 1e-06)
    gnorm_f = ratio * upstream - mixed * (ratio * ratio * ratio * inner)
    gnorm = gnorm_f.astype(BF16)
    gnorm_ref[...] = gnorm
    spread = spread_heads((gnorm_f * first).astype(BF16), own_ref)
    half = rows // 2
    early = dot_nn(gnorm[:half], values_t_ref[:, :half]).astype(BF16) * mask_ref[:half, :half]
    late = dot_nn(gnorm[half:], values_t_ref[...]).astype(BF16) * mask_ref[half:, :]
    mixing = jnp.concatenate(
        [dot_nn(early, keys_ref[:half, :]), dot_nn(late, keys_ref[...])], axis=0
    ) + dot_nt(spread, carried)
    query_grad_ref[...] = (gnorm.astype(F32) + mixing).astype(BF16)
    normed = mixed * ratio
    attended_ref[...] = (normed * gain).astype(BF16)
    gain_sum = jnp.sum(cotangent * normed, axis=0, keepdims=True)
    threshold_sum = jnp.sum(queries.astype(F32) * mixing, axis=0, keepdims=True)
    put_message(back_ref, dot_nn(queries_t_ref[...], spread), head_mark_ref)
    both = jnp.concatenate([threshold_sum / threshold_ref[...], gain_sum], axis=0)
    partial_ref[...] = jnp.broadcast_to(both[None], partial_ref.shape)


def last_kernel(
    heads, hops, scale, gnorm_ref, scores_t_ref, keys_ref, last_ref, tail_mark_ref, own_f_ref, parts_ref,
    attended_ref, query_grad_ref, *refs,
):
    received = refs[:hops]
    attended_hbm, query_grad_hbm, value_grad_hbm, threshold_hbm, gain_hbm = refs[hops : hops + 5]
    value_grad_ref, threshold_ref, gain_ref, sems = refs[hops + 5 :]
    copies = [
        pltpu.make_async_copy(attended_ref, attended_hbm, sems.at[0]),
        pltpu.make_async_copy(query_grad_ref, query_grad_hbm, sems.at[1]),
        pltpu.make_async_copy(value_grad_ref, value_grad_hbm, sems.at[2]),
        pltpu.make_async_copy(threshold_ref, threshold_hbm, sems.at[3]),
        pltpu.make_async_copy(gain_ref, gain_hbm, sems.at[4]),
    ]
    copies[0].start()
    copies[1].start()
    parts = parts_ref[...]
    even = lax.rem(row_iota(parts.shape), 2) == 0
    threshold_ref[...] = jnp.sum(jnp.where(even, parts, 0.0), axis=0, keepdims=True) * scale
    copies[3].start()
    gain_ref[...] = jnp.sum(jnp.where(even, 0.0, parts), axis=0, keepdims=True) * scale
    copies[4].start()
    returned = take_messages(received, tail_mark_ref)
    across = pick_heads(dot_nn(keys_ref[...], returned), last_ref[...], own_f_ref)
    value_grad_ref[...] = (dot_nn(scores_t_ref[...], gnorm_ref[...]) + across).astype(BF16)
    copies[2].start()
    for copy in copies:
        copy.wait()


VMEM = pl.BlockSpec(memory_space=pltpu.VMEM)
HBM = pl.BlockSpec(memory_space=pltpu.HBM)


def call(
    kernel, name, out, args, in_space=VMEM, out_spaces=None, scratch=(), flops=10**8, size=None
):
    if size is None:
        size = sum(a.size * a.dtype.itemsize for a in (*args, *out))
    return pl.pallas_call(
        kernel,
        name=name,
        out_shape=out,
        in_specs=[in_space] * len(args),
        out_specs=out_spaces or [VMEM] * len(out),
        scratch_shapes=list(scratch),
        compiler_params=pltpu.CompilerParams(vmem_limit_bytes=VMEM_LIMIT),
        cost_estimate=pl.CostEstimate(flops=flops, bytes_accessed=size, transcendentals=0),
    )(*args)


def shifted(x, by):
    count = lax.axis_size("ctx")
    pairs = [(i, (i + by) % count) for i in range(count)]
    return lax.ppermute(x, "ctx", pairs)


def neighbours(message, reach, sign):
    if reach <= 3:
        return [shifted(message, sign * by) for by in range(1, reach + 1)]
    rows = message.shape[0] - MARK_ROWS
    state, marks = message[:rows], message[rows:]
    window = 1
    while window < reach:
        other = shifted(jnp.concatenate([state, marks]), sign * window)
        same = (other[rows:][:1] == marks[:1]).astype(F32)
        state = state + same * other[:rows]
        window = 2 * window
    return [shifted(jnp.concatenate([state, marks]), sign)]


def on_device(queries, spikes, values, threshold, norm_gain, document_ids, cotangent):
    length, heads, width = queries.shape
    rows = length * heads
    blocks = lax.axis_size("ctx")
    devices = blocks * lax.axis_size("head")
    reach = -(-(length * blocks // 4 - 1) // length)
    flat = lambda x: x.reshape(rows, width)
    q, s, v, ct = flat(queries), flat(spikes), flat(values), flat(cotangent)
    thr, gain, ids = threshold[None], norm_gain[None], document_ids[None]
    like = jax.ShapeDtypeStruct
    message = like((width + MARK_ROWS, heads * width), F32)
    flat_bf = like((rows, width), BF16)
    row_f = like((1, width), F32)

    flat_f = like((rows, width), F32)
    square = like((rows, rows), BF16)
    turned = like((width, rows), BF16)
    (own,) = call(
        functools.partial(pattern_kernel, heads),
        "pattern",
        [like((heads, rows, width), BF16)],
        (),
        flops=4 * 10**9,
    )
    mark = like((MARK_ROWS, heads * width), F32)
    first, last, head_mark, tail_mark, thr = call(
        functools.partial(marks_kernel, heads), "marks", [flat_f, flat_f, mark, mark, row_f], (ids, thr),
        flops=1, size=1,
    )
    tail, keys = call(
        functools.partial(tail_kernel, heads),
        "tail",
        [message, flat_bf],
        (s, v, thr, last, tail_mark, own),
    )
    ahead = neighbours(tail, reach, 1)
    base, scores_t, mask, q_t, v_t, own_f, upstream, gain = call(
        functools.partial(inside_kernel, heads),
        "inside",
        [flat_f, square, square, turned, turned, like((heads, rows, width), F32), flat_f, row_f],
        (q, keys, v, ct, gain, ids),
    )
    attended, query_grad, gnorm, back, partial = call(
        functools.partial(middle_kernel, heads, len(ahead)),
        "middle",
        [flat_bf, flat_bf, flat_bf, message, like((devices, 2, width), F32)],
        (q, q_t, v_t, ct, upstream, base, mask, keys, thr, gain, first, head_mark, own, own_f, *ahead),
    )
    behind = neighbours(back, reach, -1)
    parts = lax.all_to_all(partial, ("ctx", "head"), 0, 0)
    scale = 1.0 / math.sqrt(rows * devices)
    attended, query_grad, value_grad, threshold_grad, gain_grad = call(
        functools.partial(last_kernel, heads, len(behind), scale),
        "last",
        [flat_bf, flat_bf, flat_bf, row_f, row_f],
        (gnorm, scores_t, keys, last, tail_mark, own_f, parts.reshape(2 * devices, width), attended, query_grad,
         *behind),
        out_spaces=[HBM] * 5,
        scratch=[pltpu.VMEM((rows, width), BF16), pltpu.VMEM((1, width), F32),
                 pltpu.VMEM((1, width), F32), pltpu.SemaphoreType.DMA((5,))],
    )
    whole = lambda x: x.reshape(length, heads, width)
    return (
        whole(attended),
        whole(query_grad),
        whole(value_grad),
        threshold_grad[0],
        gain_grad[0],
    )


def solution(mesh):
    block = P("ctx", "head", None)
    return jax.shard_map(
        on_device,
        mesh=mesh,
        in_specs=(block, block, block, P(), P(), P("ctx"), block),
        out_specs=(block, block, block, P(), P()),
        check_vma=False,
    )
```

time: 29.5 us -> 29 us (0.983)
  waiting for transfers between devices: 7.6 us -> 6.56 us
  local copies, waits for them, and re-layouts: 0.82 us -> 1.37 us
    ppermute x4, waiting for transfers between devices: 7.6 us -> 6.56 us  [shifted(): return lax.ppermute(x, 'ctx', pairs)]
    unnamed x14, local copies, waits for them, and re-layouts: 0.82 us -> 1.37 us
    pallas_call x5 -> x6, Pallas kernels: 3.48 us -> 3.39 us  [call(): pl.pallas_call(kernel, name=name, out_shape=out, in_specs=[in_space] * le...]
  transfers between devices with their start and end apart: 4 -> 4, of which waited for: 2 -> 2; matrix products, arithmetic and copies ran while one was open for 0% -> 0% of each run, Pallas kernels for 2% -> 3%
where the time goes in v4:
time: 29 us; the launch traced here: 28.8 us
  blocking collectives  10.4 us (36%)
  waiting for transfers between devices  6.56 us (23%)
  starting transfers between devices  6.33 us (22%)
  Pallas kernels  3.39 us (12%)
  local copies, waits for them, and re-layouts  1.37 us (5%)
  between operations  0.74 us (3%)
    all_to_all x1, blocking collectives, on_device(): parts = lax.all_to_all(partial, ('ctx', 'head'), 0, 0)  10.4 us
    ppermute x4, waiting for transfers between devices, shifted(): return lax.ppermute(x, 'ctx', pairs)  6.56 us
    ppermute x4, starting transfers between devices, shifted(): return lax.ppermute(x, 'ctx', pairs)  6.33 us
    pallas_call x6, Pallas kernels, call(): pl.pallas_call(kernel, name=name, out_shape=out, in_specs=[in_space] * le...  3.39 us
    unnamed x14, local copies, waits for them, and re-layouts  1.37 us
  transfers between devices with their start and end apart: 4, of which 2 were waited for; matrix products, arithmetic and copies ran while one was open for 0% of the time, Pallas kernels for 3%

profile of v4, /device:TPU:0, one launch (start us, length us, event | category | flops | bytes accessed | tf_op | source)
XLA Modules:
  0.0 28.8 jit_solution(11443103997897345996)
XLA Ops:
  0.6 0.0 copy-start
  0.6 0.0 copy-start.3
  0.7 0.1 pattern.1.own_ref
  0.7 0.0 copy-start.4
  0.8 0.0 copy-start.6
  0.8 0.7 %copy-done.4 = s32[256]{0:T(256)S(1)} copy-done((s32[256]{0:T(256)S(1)}, s32[256]{0:T(256)}, u32[]{:S(2)}) %copy-start.4) | copy-done | bytes 1048
  1.5 0.0 copy-done.6
  1.5 0.2 marks.1
  1.7 0.0 copy-start.1
  1.7 0.0 copy-start.2
  1.7 0.2 tail.1
  2.0 3.1 %collective-permute-start.1 = (f32[136,256]{1,0:T(8,128)S(1)}, f32[136,256]{1,0:T(8,128)S(1)}, u32[]{:S(2)}, u32[]{:S(2)}) collective-permute-start(f32[136,256]{1,0:T(8,128)S(1)} %get-tuple-element.43), channel_id=1, source_target_pairs={{0,8},{4,12},{8,16},{12,20},{16,24},{20,28},{24,0},{28,4},{1,9},{5... | collective-permute-start | bytes 417800 | tf_op jit(solution)/shard_map/ppermute | solution.py:218
  5.1 1.5 %collective-permute-start = (f32[136,256]{1,0:T(8,128)S(1)}, f32[136,256]{1,0:T(8,128)S(1)}, u32[]{:S(2)}, u32[]{:S(2)}) collective-permute-start(f32[136,256]{1,0:T(8,128)S(1)} %get-tuple-element.43), channel_id=1, source_target_pairs={{0,4},{4,8},{8,12},{12,16},{16,20},{20,24},{24,28},{28,0},{1,5},{5... | collective-permute-start | bytes 417800 | tf_op jit(solution)/shard_map/ppermute | solution.py:218
  6.6 0.6 %copy-done.5 = f32[128]{0:T(128)S(1)} copy-done((f32[128]{0:T(128)S(1)}, f32[128]{0:T(128)}, u32[]{:S(2)}) %copy-start.5) | copy-done | bytes 536
  7.2 0.9 %inside.1 = (f32[512,128]{1,0:T(8,128)S(1)}, bf16[512,512]{1,0:T(8,128)(2,1)S(1)}, bf16[512,512]{1,0:T(8,128)(2,1)S(1)}, bf16[128,512]{1,0:T(8,128)(2,1)S(1)}, b...) custom-call(bf16[512,128]{1,0:T(8,128)(2,1)S(1)} %bitcast.15, ...), custom_call_target="tpu_custom_call" | custom-call | flops 100000000 | bytes 2885632 | tf_op jit(solution)/shard_map/inside/pallas_call | solution.py:203
  8.2 2.6 %collective-permute-done.1.refs_1_ = f32[136,256]{1,0:T(8,128)S(1)} collective-permute-done((f32[136,256]{1,0:T(8,128)S(1)}, f32[136,256]{1,0:T(8,128)S(1)}, u32[]{:S(2)}, u32[]{:S(2)}) %collective-permute-start.1) | collective-permute-done | bytes 139296 | tf_op jit(solution)/shard_map/ppermute | solution.py:218
  10.8 3.9 %collective-permute-done.refs_0_ = f32[136,256]{1,0:T(8,128)S(1)} collective-permute-done((f32[136,256]{1,0:T(8,128)S(1)}, f32[136,256]{1,0:T(8,128)S(1)}, u32[]{:S(2)}, u32[]{:S(2)}) %collective-permute-start) | collective-permute-done | bytes 139296 | tf_op jit(solution)/shard_map/ppermute | solution.py:218
  14.7 0.8 %middle.1 = (bf16[512,128]{1,0:T(8,128)(2,1)S(1)}, bf16[512,128]{1,0:T(8,128)(2,1)S(1)}, bf16[512,128]{1,0:T(8,128)(2,1)S(1)}, f32[136,256]{1,0:T(8,128)S(1)}, f32[32,2,128]{2,1,0:T(2,128)S(1)}) custom-call(bf16[512,128]{1,0:T(8,128)(2,1)S(1)} %bitcast.16, bf16[128,512]{1,0:T(8,128)(2,1)S(1)} %get-tuple-element.34.queries_t_ref, ...), custom_call_target="tpu_custom_call" | custom-call | flops 100000000 | bytes 3605504 | tf_op jit(solution)/shard_map/middle/pallas_call | solution.py:203
  15.5 1.8 %collective-permute-start.3 = (f32[136,256]{1,0:T(8,128)S(1)}, f32[136,256]{1,0:T(8,128)S(1)}, u32[]{:S(2)}, u32[]{:S(2)}) collective-permute-start(f32[136,256]{1,0:T(8,128)S(1)} %get-tuple-element.49), channel_id=1, source_target_pairs={{0,24},{4,28},{8,0},{12,4},{16,8},{20,12},{24,16},{28,20},{1,25},{... | collective-permute-start | bytes 417800 | tf_op jit(solution)/shard_map/ppermute | solution.py:218
  17.3 0.0 collective-permute-start.2
  17.3 10.4 %all_to_all.5 = f32[32,2,128]{2,1,0:T(2,128)S(1)} all-to-all(f32[32,2,128]{2,1,0:T(2,128)S(1)} %get-tuple-element.46), channel_id=1, replica_groups=mesh['ctx'=8,'head'=4] {'ctx','head'}, dimensions={0} | all-to-all | bytes 65536 | tf_op jit(solution)/shard_map/all_to_all | solution.py:284
  27.7 0.0 collective-permute-done.3.refs_1_
  27.7 0.0 collective-permute-done.2.refs_0_
  27.7 1.1 %last.1 = (bf16[512,128]{1,0:T(8,128)(2,1)}, bf16[512,128]{1,0:T(8,128)(2,1)}, bf16[512,128]{1,0:T(8,128)(2,1)}, f32[1,128]{1,0:T(1,128)}, f32[1,128]{1,0:T(1,128)}) custom-call(bf16[512,128]{1,0:T(8,128)(2,1)S(1)} %get-tuple-element.44.gnorm_ref, bf16[512,512]{1,0:T(8,128)(2,1)S(1)} %get-tuple-element.45.scores_t_ref, ...), custom_call_target="tpu_custom_call" | custom-call | flops 100000000 | bytes 2548736 | tf_op jit(solution)/shard_map/last/pallas_call | solution.py:203
  (5 shorter events, 0.0 us)
Async XLA Ops:
  0.6 1.1 %copy-start = (bf16[256,2,128]{2,1,0:T(2,128)(2,1)S(1)}, bf16[256,2,128]{2,1,0:T(2,128)(2,1)}, u32[]{:S(2)}) copy-start(bf16[256,2,128]{2,1,0:T(2,128)(2,1)} %param.9) | copy-start | bytes 393220
  0.6 1.1 %copy-start.3 = (s32[256,2,128]{2,1,0:T(2,128)S(1)}, s32[256,2,128]{2,1,0:T(2,128)}, u32[]{:S(2)}) copy-start(s32[256,2,128]{2,1,0:T(2,128)} %param.8) | copy-start | bytes 786436
  0.7 0.7 %copy-start.4 = (s32[256]{0:T(256)S(1)}, s32[256]{0:T(256)}, u32[]{:S(2)}) copy-start(s32[256]{0:T(256)} %param.12) | copy-start | bytes 3076
  0.8 0.7 %copy-start.6 = (f32[128]{0:T(128)S(1)}, f32[128]{0:T(128)}, u32[]{:S(2)}) copy-start(f32[128]{0:T(128)} %param.10) | copy-start | bytes 1540
  1.7 4.8 %copy-start.1 = (bf16[256,2,128]{2,1,0:T(2,128)(2,1)S(1)}, bf16[256,2,128]{2,1,0:T(2,128)(2,1)}, u32[]{:S(2)}) copy-start(bf16[256,2,128]{2,1,0:T(2,128)(2,1)} %param.7) | copy-start | bytes 393220
  1.7 4.8 %copy-start.2 = (bf16[256,2,128]{2,1,0:T(2,128)(2,1)S(1)}, bf16[256,2,128]{2,1,0:T(2,128)(2,1)}, u32[]{:S(2)}) copy-start(bf16[256,2,128]{2,1,0:T(2,128)(2,1)} %param.13) | copy-start | bytes 393220
  2.0 8.8 %collective-permute-start.1 = (f32[136,256]{1,0:T(8,128)S(1)}, f32[136,256]{1,0:T(8,128)S(1)}, u32[]{:S(2)}, u32[]{:S(2)}) collective-permute-start(f32[136,256]{1,0:T(8,128)S(1)} %get-tuple-element.43), channel_id=1, source_target_pairs={{0,8},{4,12},{8,16},{12,20},{16,24},{20,28},{24,0},{28,4},{1,9},{5... | collective-permute-start | bytes 417800 | tf_op jit(solution)/shard_map/ppermute | solution.py:218
  5.1 9.6 %collective-permute-start = (f32[136,256]{1,0:T(8,128)S(1)}, f32[136,256]{1,0:T(8,128)S(1)}, u32[]{:S(2)}, u32[]{:S(2)}) collective-permute-start(f32[136,256]{1,0:T(8,128)S(1)} %get-tuple-element.43), channel_id=1, source_target_pairs={{0,4},{4,8},{8,12},{12,16},{16,20},{20,24},{24,28},{28,0},{1,5},{5... | collective-permute-start | bytes 417800 | tf_op jit(solution)/shard_map/ppermute | solution.py:218
  6.6 0.7 %copy-start.5 = (f32[128]{0:T(128)S(1)}, f32[128]{0:T(128)}, u32[]{:S(2)}) copy-start(f32[128]{0:T(128)} %param.11) | copy-start | bytes 1540
  15.5 12.2 %collective-permute-start.3 = (f32[136,256]{1,0:T(8,128)S(1)}, f32[136,256]{1,0:T(8,128)S(1)}, u32[]{:S(2)}, u32[]{:S(2)}) collective-permute-start(f32[136,256]{1,0:T(8,128)S(1)} %get-tuple-element.49), channel_id=1, source_target_pairs={{0,24},{4,28},{8,0},{12,4},{16,8},{20,12},{24,16},{28,20},{1,25},{... | collective-permute-start | bytes 417800 | tf_op jit(solution)/shard_map/ppermute | solution.py:218
  17.3 10.4 %collective-permute-start.2 = (f32[136,256]{1,0:T(8,128)S(1)}, f32[136,256]{1,0:T(8,128)S(1)}, u32[]{:S(2)}, u32[]{:S(2)}) collective-permute-start(f32[136,256]{1,0:T(8,128)S(1)} %get-tuple-element.49), channel_id=1, source_target_pairs={{0,28},{4,0},{8,4},{12,8},{16,12},{20,16},{24,20},{28,24},{1,29},{... | collective-permute-start | bytes 417800 | tf_op jit(solution)/shard_map/ppermute | solution.py:218

commit v5 on v4

--- a/solution.py
+++ b/solution.py
@@ -38,18 +38,11 @@
     return jnp.concatenate([x * own_ref[h] for h in range(own_ref.shape[0])], axis=1)
 
 
-def pick_heads(x, keep, own_ref):
-    heads, _, width = own_ref.shape
-    out = x[:, :width]
-    for h in range(1, heads):
-        out = jnp.where(own_ref[h] > 0, x[:, h * width : (h + 1) * width], out)
-    return out * keep
-
-
 def put_message(out_ref, state, mark_ref):
-    count = state.shape[0]
-    out_ref[:count, :] = state
-    out_ref[count:, :] = mark_ref[...]
+    count, width = state.shape[0], out_ref.shape[1]
+    for h in range(state.shape[1] // width):
+        out_ref[h * count : (h + 1) * count, :] = state[:, h * width : (h + 1) * width]
+    out_ref[out_ref.shape[0] - MARK_ROWS :, :] = mark_ref[...]
 
 
 def take_messages(refs, mark_ref):
@@ -62,6 +55,11 @@
     return total.astype(BF16)
 
 
+def side_by_side(state, heads):
+    count = state.shape[0] // heads
+    return jnp.concatenate([state[h * count : (h + 1) * count] for h in range(heads)], axis=1)
+
+
 def pattern_kernel(heads, own_ref):
     head = lax.rem(row_iota(own_ref.shape[1:]), heads)
     for h in range(heads):
@@ -69,17 +67,13 @@
 
 
 def marks_kernel(
-    heads, ids_ref, threshold_ref, first_ref, last_ref, head_mark_ref, tail_mark_ref, threshold_out_ref
+    heads, ids_ref, threshold_ref, last_ref, tail_mark_ref, threshold_out_ref
 ):
     threshold_out_ref[...] = threshold_ref[...]
     ids = ids_ref[...]
-    head, tail = ids[:, :1], ids[:, ids.shape[1] - 1 :]
-    in_first = jnp.sum((ids == head).astype(jnp.int32), axis=1, keepdims=True)
+    tail = ids[:, ids.shape[1] - 1 :]
     before_last = jnp.sum((ids != tail).astype(jnp.int32), axis=1, keepdims=True)
-    row = row_iota(first_ref.shape)
-    first_ref[...] = (row < heads * in_first).astype(F32)
-    last_ref[...] = (row >= heads * before_last).astype(F32)
-    head_mark_ref[...] = jnp.broadcast_to(head.astype(F32), head_mark_ref.shape)
+    last_ref[...] = (row_iota(last_ref.shape) >= heads * before_last).astype(F32)
     tail_mark_ref[...] = jnp.broadcast_to(tail.astype(F32), tail_mark_ref.shape)
 
 
@@ -93,13 +87,19 @@
 
 
 def inside_kernel(
-    heads, queries_ref, keys_ref, values_ref, cotangent_ref, gain_ref, ids_ref,
-    base_ref, scores_t_ref, mask_ref, queries_t_ref, values_t_ref, own_ref, upstream_ref, gain_out_ref,
+    heads, queries_ref, keys_ref, values_ref, cotangent_ref, gain_ref, ids_ref, last_ref, own_ref,
+    first_ref, head_mark_ref, base_ref, scores_t_ref, mask_ref, values_t_ref, first_queries_ref,
+    first_queries_t_ref, last_keys_ref, upstream_ref, gain_out_ref,
 ):
     rows = queries_ref.shape[0]
     tokens = ids_ref.shape[1]
     queries = queries_ref[...]
     ids = ids_ref[...].astype(F32)
+    head = ids[:, :1]
+    in_first = jnp.sum((ids == head).astype(jnp.int32), axis=1, keepdims=True)
+    first = (row_iota(first_ref.shape) < heads * in_first).astype(F32)
+    first_ref[...] = first
+    head_mark_ref[...] = jnp.broadcast_to(head, head_mark_ref.shape)
     apart = row_iota((rows, tokens)) - heads * col_iota((rows, tokens))
     down = jnp.sum(
         jnp.where((apart >= 0) & (apart < heads), ids, 0.0), axis=1, keepdims=True
@@ -114,19 +114,22 @@
     scores = dot_nt(queries, keys).astype(BF16) * allowed
     scores_t_ref[...] = dot_nt(keys, queries).astype(BF16) * allowed_t
     mask_ref[...] = allowed
-    queries_t_ref[...] = queries.T
     values_t_ref[...] = values_ref[...].T
-    head = lax.rem(row_iota(own_ref.shape[1:]), heads)
-    for h in range(heads):
-        own_ref[h] = (head == h).astype(F32)
+    first_queries = spread_heads(
+        (queries.astype(F32) * first).astype(BF16), own_ref
+    )
+    first_queries_ref[...] = first_queries
+    first_queries_t_ref[...] = first_queries.T
+    last_keys_ref[...] = spread_heads((keys.astype(F32) * last_ref[...]).astype(BF16), own_ref)
     gain_out_ref[...] = gain_ref[...]
     upstream_ref[...] = cotangent_ref[...].astype(F32) * gain_ref[...]
     base_ref[...] = queries.astype(F32) + dot_nn(scores, values_ref[...])
 
 
 def middle_kernel(
-    heads, hops, queries_ref, queries_t_ref, values_t_ref, cotangent_ref, upstream_ref, base_ref, mask_ref, keys_ref,
-    threshold_ref, gain_ref, first_ref, head_mark_ref, own_ref, own_f_ref, *refs,
+    heads, hops, queries_ref, first_queries_ref, first_queries_t_ref, values_t_ref, cotangent_ref,
+    upstream_ref, base_ref, mask_ref, keys_ref, threshold_ref, gain_ref, first_ref, head_mark_ref,
+    own_ref, *refs,
 ):
     received = refs[:hops]
     attended_ref, query_grad_ref, gnorm_ref, back_ref, partial_ref = refs[hops:]
@@ -135,7 +138,7 @@
     gain = gain_ref[...]
     first = first_ref[...]
     queries = queries_ref[...]
-    mixed = base_ref[...] + pick_heads(dot_nn(queries, carried), first, own_f_ref)
+    mixed = base_ref[...] + dot_nn(first_queries_ref[...], carried)
     cotangent = cotangent_ref[...].astype(F32)
     upstream = upstream_ref[...]
     square = jnp.mean(mixed * mixed, axis=1, keepdims=True)
@@ -150,19 +153,19 @@
     late = dot_nn(gnorm[half:], values_t_ref[...]).astype(BF16) * mask_ref[half:, :]
     mixing = jnp.concatenate(
         [dot_nn(early, keys_ref[:half, :]), dot_nn(late, keys_ref[...])], axis=0
-    ) + dot_nt(spread, carried)
+    ) + dot_nt(spread, side_by_side(carried, heads))
     query_grad_ref[...] = (gnorm.astype(F32) + mixing).astype(BF16)
     normed = mixed * ratio
     attended_ref[...] = (normed * gain).astype(BF16)
     gain_sum = jnp.sum(cotangent * normed, axis=0, keepdims=True)
     threshold_sum = jnp.sum(queries.astype(F32) * mixing, axis=0, keepdims=True)
-    put_message(back_ref, dot_nn(queries_t_ref[...], spread), head_mark_ref)
+    put_message(back_ref, dot_nn(first_queries_t_ref[...], gnorm), head_mark_ref)
     both = jnp.concatenate([threshold_sum / threshold_ref[...], gain_sum], axis=0)
     partial_ref[...] = jnp.broadcast_to(both[None], partial_ref.shape)
 
 
 def last_kernel(
-    heads, hops, scale, gnorm_ref, scores_t_ref, keys_ref, last_ref, tail_mark_ref, own_f_ref, parts_ref,
+    heads, hops, scale, gnorm_ref, scores_t_ref, last_keys_ref, tail_mark_ref, parts_ref,
     attended_ref, query_grad_ref, *refs,
 ):
     received = refs[:hops]
@@ -184,7 +187,7 @@
     gain_ref[...] = jnp.sum(jnp.where(even, 0.0, parts), axis=0, keepdims=True) * scale
     copies[4].start()
     returned = take_messages(received, tail_mark_ref)
-    across = pick_heads(dot_nn(keys_ref[...], returned), last_ref[...], own_f_ref)
+    across = dot_nn(last_keys_ref[...], returned)
     value_grad_ref[...] = (dot_nn(scores_t_ref[...], gnorm_ref[...]) + across).astype(BF16)
     copies[2].start()
     for copy in copies:
@@ -220,7 +223,8 @@
 
 def neighbours(message, reach, sign):
     if reach <= 3:
-        return [shifted(message, sign * by) for by in range(1, reach + 1)]
+        order = range(reach, 0, -1) if sign > 0 else range(1, reach + 1)
+        return [shifted(message, sign * by) for by in order]
     rows = message.shape[0] - MARK_ROWS
     state, marks = message[:rows], message[rows:]
     window = 1
@@ -242,13 +246,12 @@
     q, s, v, ct = flat(queries), flat(spikes), flat(values), flat(cotangent)
     thr, gain, ids = threshold[None], norm_gain[None], document_ids[None]
     like = jax.ShapeDtypeStruct
-    message = like((width + MARK_ROWS, heads * width), F32)
+    message = like((heads * width + MARK_ROWS, width), F32)
     flat_bf = like((rows, width), BF16)
     row_f = like((1, width), F32)
 
     flat_f = like((rows, width), F32)
     square = like((rows, rows), BF16)
-    turned = like((width, rows), BF16)
     (own,) = call(
         functools.partial(pattern_kernel, heads),
         "pattern",
@@ -256,9 +259,9 @@
         (),
         flops=4 * 10**9,
     )
-    mark = like((MARK_ROWS, heads * width), F32)
-    first, last, head_mark, tail_mark, thr = call(
-        functools.partial(marks_kernel, heads), "marks", [flat_f, flat_f, mark, mark, row_f], (ids, thr),
+    mark = like((MARK_ROWS, width), F32)
+    last, tail_mark, thr = call(
+        functools.partial(marks_kernel, heads), "marks", [flat_f, mark, row_f], (ids, thr),
         flops=1, size=1,
     )
     tail, keys = call(
@@ -268,26 +271,29 @@
         (s, v, thr, last, tail_mark, own),
     )
     ahead = neighbours(tail, reach, 1)
-    base, scores_t, mask, q_t, v_t, own_f, upstream, gain = call(
+    wide = like((rows, heads * width), BF16)
+    first, head_mark, base, scores_t, mask, v_t, first_q, first_q_t, last_k, upstream, gain = call(
         functools.partial(inside_kernel, heads),
         "inside",
-        [flat_f, square, square, turned, turned, like((heads, rows, width), F32), flat_f, row_f],
-        (q, keys, v, ct, gain, ids),
+        [flat_f, mark, flat_f, square, square, like((width, rows), BF16), wide, like((heads * width, rows), BF16),
+         wide, flat_f, row_f],
+        (q, keys, v, ct, gain, ids, last, own),
     )
     attended, query_grad, gnorm, back, partial = call(
         functools.partial(middle_kernel, heads, len(ahead)),
         "middle",
         [flat_bf, flat_bf, flat_bf, message, like((devices, 2, width), F32)],
-        (q, q_t, v_t, ct, upstream, base, mask, keys, thr, gain, first, head_mark, own, own_f, *ahead),
+        (q, first_q, first_q_t, v_t, ct, upstream, base, mask, keys, thr, gain, first, head_mark, own,
+         *ahead),
     )
     behind = neighbours(back, reach, -1)
-    parts = lax.all_to_all(partial, ("ctx", "head"), 0, 0)
+    parts = lax.all_to_all(partial, ("head", "ctx"), 0, 0)
     scale = 1.0 / math.sqrt(rows * devices)
     attended, query_grad, value_grad, threshold_grad, gain_grad = call(
         functools.partial(last_kernel, heads, len(behind), scale),
         "last",
         [flat_bf, flat_bf, flat_bf, row_f, row_f],
-        (gnorm, scores_t, keys, last, tail_mark, own_f, parts.reshape(2 * devices, width), attended, query_grad,
+        (gnorm, scores_t, last_k, tail_mark, parts.reshape(2 * devices, width), attended, query_grad,
          *behind),
         out_spaces=[HBM] * 5,
         scratch=[pltpu.VMEM((rows, width), BF16), pltpu.VMEM((1, width), F32),

time: 29 us -> 28.7 us (0.990)
  starting transfers between devices: 6.33 us -> 8.85 us
  waiting for transfers between devices: 6.56 us -> 4.22 us
  blocking collectives: 10.4 us -> 9.88 us
    ppermute x4, starting transfers between devices: 6.33 us -> 8.85 us  [shifted(): return lax.ppermute(x, 'ctx', pairs)]
    ppermute x4, waiting for transfers between devices: 6.56 us -> 4.22 us  [shifted(): return lax.ppermute(x, 'ctx', pairs)]
    all_to_all x1, blocking collectives: 10.4 us -> 9.88 us  [on_device(): parts = lax.all_to_all(partial, ('head', 'ctx'), 0, 0)]
  transfers between devices with their start and end apart: 4 -> 4, of which waited for: 2 -> 1; matrix products, arithmetic and copies ran while one was open for 0% -> 0% of each run, Pallas kernels for 3% -> 4%
where the time goes in v5:
time: 28.7 us; the launch traced here: 28.5 us
  blocking collectives  9.88 us (34%)
  starting transfers between devices  8.85 us (31%)
  waiting for transfers between devices  4.22 us (15%)
  Pallas kernels  3.45 us (12%)
  local copies, waits for them, and re-layouts  1.37 us (5%)
  between operations  0.74 us (3%)
    all_to_all x1, blocking collectives, on_device(): parts = lax.all_to_all(partial, ('head', 'ctx'), 0, 0)  9.88 us
    ppermute x4, starting transfers between devices, shifted(): return lax.ppermute(x, 'ctx', pairs)  8.85 us
    ppermute x4, waiting for transfers between devices, shifted(): return lax.ppermute(x, 'ctx', pairs)  4.22 us
    pallas_call x6, Pallas kernels, call(): pl.pallas_call(kernel, name=name, out_shape=out, in_specs=[in_space] * le...  3.45 us
    unnamed x14, local copies, waits for them, and re-layouts  1.37 us
  transfers between devices with their start and end apart: 4, of which 1 were waited for; matrix products, arithmetic and copies ran while one was open for 0% of the time, Pallas kernels for 4%

profile of v5, /device:TPU:0, one launch (start us, length us, event | category | flops | bytes accessed | tf_op | source)
XLA Modules:
  0.0 28.5 jit_solution(8248723646256059183)
XLA Ops:
  0.6 0.0 copy-start
  0.6 0.0 copy-start.3
  0.7 0.1 pattern.1.own_ref
  0.7 0.0 copy-start.4
  0.8 0.0 copy-start.6
  0.8 0.7 %copy-done.4 = s32[256]{0:T(256)S(1)} copy-done((s32[256]{0:T(256)S(1)}, s32[256]{0:T(256)}, u32[]{:S(2)}) %copy-start.4) | copy-done | bytes 1048
  1.5 0.0 copy-done.6
  1.5 0.2 marks.1
  1.7 0.0 copy-start.1
  1.7 0.0 copy-start.2
  1.7 0.2 tail.1
  1.9 3.0 %collective-permute-start.1 = (f32[264,128]{1,0:T(8,128)S(1)}, f32[264,128]{1,0:T(8,128)S(1)}, u32[]{:S(2)}, u32[]{:S(2)}) collective-permute-start(f32[264,128]{1,0:T(8,128)S(1)} %get-tuple-element.44), channel_id=1, source_target_pairs={{0,4},{4,8},{8,12},{12,16},{16,20},{20,24},{24,28},{28,0},{1,5},{5... | collective-permute-start | bytes 405512 | tf_op jit(solution)/shard_map/ppermute | solution.py:221
  4.9 1.6 %collective-permute-start = (f32[264,128]{1,0:T(8,128)S(1)}, f32[264,128]{1,0:T(8,128)S(1)}, u32[]{:S(2)}, u32[]{:S(2)}) collective-permute-start(f32[264,128]{1,0:T(8,128)S(1)} %get-tuple-element.44), channel_id=1, source_target_pairs={{0,8},{4,12},{8,16},{12,20},{16,24},{20,28},{24,0},{28,4},{1,9},{5... | collective-permute-start | bytes 405512 | tf_op jit(solution)/shard_map/ppermute | solution.py:221
  6.5 0.6 %copy-done.5 = f32[128]{0:T(128)S(1)} copy-done((f32[128]{0:T(128)S(1)}, f32[128]{0:T(128)}, u32[]{:S(2)}) %copy-start.5) | copy-done | bytes 536
  7.2 1.0 %inside.1 = (f32[512,128]{1,0:T(8,128)S(1)}, f32[8,128]{1,0:T(8,128)S(1)}, f32[512,128]{1,0:T(8,128)S(1)}, bf16[512,512]{1,0:T(8,128)(2,1)S(1)}, bf16[512,512]{1...) custom-call(bf16[512,128]{1,0:T(8,128)(2,1)S(1)} %bitcast.15, ...), custom_call_target="tpu_custom_call" | custom-call | flops 100000000 | bytes 3807232 | tf_op jit(solution)/shard_map/inside/pallas_call | solution.py:206
  8.2 4.2 %collective-permute-done.1.refs_1_ = f32[264,128]{1,0:T(8,128)S(1)} collective-permute-done((f32[264,128]{1,0:T(8,128)S(1)}, f32[264,128]{1,0:T(8,128)S(1)}, u32[]{:S(2)}, u32[]{:S(2)}) %collective-permute-start.1) | collective-permute-done | bytes 135200 | tf_op jit(solution)/shard_map/ppermute | solution.py:221
  12.4 0.0 collective-permute-done.refs_0_
  12.4 0.8 %middle.1 = (bf16[512,128]{1,0:T(8,128)(2,1)S(1)}, bf16[512,128]{1,0:T(8,128)(2,1)S(1)}, bf16[512,128]{1,0:T(8,128)(2,1)S(1)}, f32[264,128]{1,0:T(8,128)S(1)}, f32[32,2,128]{2,1,0:T(2,128)S(1)}) custom-call(bf16[512,128]{1,0:T(8,128)(2,1)S(1)} %bitcast.16, bf16[512,256]{1,0:T(8,128)(2,1)S(1)} %get-tuple-element.35.first_queries_ref, ...), custom_call_target="tpu_custom_call" | custom-call | flops 100000000 | bytes 3458048 | tf_op jit(solution)/shard_map/middle/pallas_call | solution.py:206
  13.2 2.1 %collective-permute-start.3 = (f32[264,128]{1,0:T(8,128)S(1)}, f32[264,128]{1,0:T(8,128)S(1)}, u32[]{:S(2)}, u32[]{:S(2)}) collective-permute-start(f32[264,128]{1,0:T(8,128)S(1)} %get-tuple-element.51), channel_id=1, source_target_pairs={{0,24},{4,28},{8,0},{12,4},{16,8},{20,12},{24,16},{28,20},{1,25},{... | collective-permute-start | bytes 405512 | tf_op jit(solution)/shard_map/ppermute | solution.py:221
  15.3 2.2 %collective-permute-start.2 = (f32[264,128]{1,0:T(8,128)S(1)}, f32[264,128]{1,0:T(8,128)S(1)}, u32[]{:S(2)}, u32[]{:S(2)}) collective-permute-start(f32[264,128]{1,0:T(8,128)S(1)} %get-tuple-element.51), channel_id=1, source_target_pairs={{0,28},{4,0},{8,4},{12,8},{16,12},{20,16},{24,20},{28,24},{1,29},{... | collective-permute-start | bytes 405512 | tf_op jit(solution)/shard_map/ppermute | solution.py:221
  17.5 9.9 %all_to_all.5 = f32[32,2,128]{2,1,0:T(2,128)S(1)} all-to-all(f32[32,2,128]{2,1,0:T(2,128)S(1)} %get-tuple-element.48), channel_id=1, replica_groups=mesh['ctx'=8,'head'=4] {'head','ctx'}, dimensions={0} | all-to-all | bytes 65536 | tf_op jit(solution)/shard_map/all_to_all | solution.py:290
  27.4 0.0 collective-permute-done.3.refs_1_
  27.4 0.0 collective-permute-done.2.refs_0_
  27.4 1.1 %last.1 = (bf16[512,128]{1,0:T(8,128)(2,1)}, bf16[512,128]{1,0:T(8,128)(2,1)}, bf16[512,128]{1,0:T(8,128)(2,1)}, f32[1,128]{1,0:T(1,128)}, f32[1,128]{1,0:T(1,128)}) custom-call(bf16[512,128]{1,0:T(8,128)(2,1)S(1)} %get-tuple-element.45.gnorm_ref, bf16[512,512]{1,0:T(8,128)(2,1)S(1)} %get-tuple-element.46.scores_t_ref, ...), custom_call_target="tpu_custom_call" | custom-call | flops 100000000 | bytes 1881088 | tf_op jit(solution)/shard_map/last/pallas_call | solution.py:206
  (5 shorter events, 0.0 us)
Async XLA Ops:
  0.6 1.0 %copy-start = (bf16[256,2,128]{2,1,0:T(2,128)(2,1)S(1)}, bf16[256,2,128]{2,1,0:T(2,128)(2,1)}, u32[]{:S(2)}) copy-start(bf16[256,2,128]{2,1,0:T(2,128)(2,1)} %param.9) | copy-start | bytes 393220
  0.6 1.0 %copy-start.3 = (s32[256,2,128]{2,1,0:T(2,128)S(1)}, s32[256,2,128]{2,1,0:T(2,128)}, u32[]{:S(2)}) copy-start(s32[256,2,128]{2,1,0:T(2,128)} %param.8) | copy-start | bytes 786436
  0.7 0.7 %copy-start.4 = (s32[256]{0:T(256)S(1)}, s32[256]{0:T(256)}, u32[]{:S(2)}) copy-start(s32[256]{0:T(256)} %param.12) | copy-start | bytes 3076
  0.8 0.7 %copy-start.6 = (f32[128]{0:T(128)S(1)}, f32[128]{0:T(128)}, u32[]{:S(2)}) copy-start(f32[128]{0:T(128)} %param.10) | copy-start | bytes 1540
  1.7 4.8 %copy-start.1 = (bf16[256,2,128]{2,1,0:T(2,128)(2,1)S(1)}, bf16[256,2,128]{2,1,0:T(2,128)(2,1)}, u32[]{:S(2)}) copy-start(bf16[256,2,128]{2,1,0:T(2,128)(2,1)} %param.7) | copy-start | bytes 393220
  1.7 4.8 %copy-start.2 = (bf16[256,2,128]{2,1,0:T(2,128)(2,1)S(1)}, bf16[256,2,128]{2,1,0:T(2,128)(2,1)}, u32[]{:S(2)}) copy-start(bf16[256,2,128]{2,1,0:T(2,128)(2,1)} %param.13) | copy-start | bytes 393220
  1.9 10.4 %collective-permute-start.1 = (f32[264,128]{1,0:T(8,128)S(1)}, f32[264,128]{1,0:T(8,128)S(1)}, u32[]{:S(2)}, u32[]{:S(2)}) collective-permute-start(f32[264,128]{1,0:T(8,128)S(1)} %get-tuple-element.44), channel_id=1, source_target_pairs={{0,4},{4,8},{8,12},{12,16},{16,20},{20,24},{24,28},{28,0},{1,5},{5... | collective-permute-start | bytes 405512 | tf_op jit(solution)/shard_map/ppermute | solution.py:221
  4.9 7.5 %collective-permute-start = (f32[264,128]{1,0:T(8,128)S(1)}, f32[264,128]{1,0:T(8,128)S(1)}, u32[]{:S(2)}, u32[]{:S(2)}) collective-permute-start(f32[264,128]{1,0:T(8,128)S(1)} %get-tuple-element.44), channel_id=1, source_target_pairs={{0,8},{4,12},{8,16},{12,20},{16,24},{20,28},{24,0},{28,4},{1,9},{5... | collective-permute-start | bytes 405512 | tf_op jit(solution)/shard_map/ppermute | solution.py:221
  6.5 0.7 %copy-start.5 = (f32[128]{0:T(128)S(1)}, f32[128]{0:T(128)}, u32[]{:S(2)}) copy-start(f32[128]{0:T(128)} %param.11) | copy-start | bytes 1540
  13.2 14.2 %collective-permute-start.3 = (f32[264,128]{1,0:T(8,128)S(1)}, f32[264,128]{1,0:T(8,128)S(1)}, u32[]{:S(2)}, u32[]{:S(2)}) collective-permute-start(f32[264,128]{1,0:T(8,128)S(1)} %get-tuple-element.51), channel_id=1, source_target_pairs={{0,24},{4,28},{8,0},{12,4},{16,8},{20,12},{24,16},{28,20},{1,25},{... | collective-permute-start | bytes 405512 | tf_op jit(solution)/shard_map/ppermute | solution.py:221
  15.3 12.1 %collective-permute-start.2 = (f32[264,128]{1,0:T(8,128)S(1)}, f32[264,128]{1,0:T(8,128)S(1)}, u32[]{:S(2)}, u32[]{:S(2)}) collective-permute-start(f32[264,128]{1,0:T(8,128)S(1)} %get-tuple-element.51), channel_id=1, source_target_pairs={{0,28},{4,0},{8,4},{12,8},{16,12},{20,16},{24,20},{28,24},{1,29},{... | collective-permute-start | bytes 405512 | tf_op jit(solution)/shard_map/ppermute | solution.py:221

commit v6 on v5

--- a/solution.py
+++ b/solution.py
@@ -216,9 +216,15 @@
 
 
 def shifted(x, by):
-    count = lax.axis_size("ctx")
-    pairs = [(i, (i + by) % count) for i in range(count)]
-    return lax.ppermute(x, "ctx", pairs)
+    count, lanes = lax.axis_size("ctx"), lax.axis_size("head")
+    pairs = []
+    for block in range(count):
+        for lane in range(lanes):
+            wraps = not 0 <= block + by < count
+            swap = wraps and abs(by) == 2 and lanes % 2 == 0
+            to = (block + by) % count * lanes + (lane ^ 1 if swap else lane)
+            pairs.append((block * lanes + lane, to))
+    return lax.ppermute(x, ("ctx", "head"), pairs)
 
 
 def neighbours(message, reach, sign):

time: 28.7 us -> 28.1 us (0.979)
  blocking collectives: 9.88 us -> 9.32 us
    all_to_all x1, blocking collectives: 9.88 us -> 9.32 us  [on_device(): parts = lax.all_to_all(partial, ('head', 'ctx'), 0, 0)]
where the time goes in v6:
time: 28.1 us; the launch traced here: 27.9 us
  blocking collectives  9.32 us (33%)
  starting transfers between devices  8.84 us (31%)
  waiting for transfers between devices  4.22 us (15%)
  Pallas kernels  3.45 us (12%)
  local copies, waits for them, and re-layouts  1.37 us (5%)
  between operations  0.74 us (3%)
    all_to_all x1, blocking collectives, on_device(): parts = lax.all_to_all(partial, ('head', 'ctx'), 0, 0)  9.32 us
    ppermute x4, starting transfers between devices, shifted(): return lax.ppermute(x, ('ctx', 'head'), pairs)  8.84 us
    ppermute x4, waiting for transfers between devices, shifted(): return lax.ppermute(x, ('ctx', 'head'), pairs)  4.22 us
    pallas_call x6, Pallas kernels, call(): pl.pallas_call(kernel, name=name, out_shape=out, in_specs=[in_space] * le...  3.45 us
    unnamed x14, local copies, waits for them, and re-layouts  1.37 us
  transfers between devices with their start and end apart: 4, of which 1 were waited for; matrix products, arithmetic and copies ran while one was open for 0% of the time, Pallas kernels for 4%

profile of v6, /device:TPU:0, one launch (start us, length us, event | category | flops | bytes accessed | tf_op | source)
XLA Modules:
  0.0 27.9 jit_solution(2040899602796138850)
XLA Ops:
  0.6 0.0 copy-start
  0.6 0.0 copy-start.3
  0.7 0.1 pattern.1.own_ref
  0.7 0.0 copy-start.4
  0.8 0.0 copy-start.6
  0.8 0.7 %copy-done.4 = s32[256]{0:T(256)S(1)} copy-done((s32[256]{0:T(256)S(1)}, s32[256]{0:T(256)}, u32[]{:S(2)}) %copy-start.4) | copy-done | bytes 1048
  1.5 0.0 copy-done.6
  1.5 0.2 marks.1
  1.7 0.0 copy-start.1
  1.7 0.0 copy-start.2
  1.7 0.2 tail.1
  1.9 3.0 %collective-permute-start.1 = (f32[264,128]{1,0:T(8,128)S(1)}, f32[264,128]{1,0:T(8,128)S(1)}, u32[]{:S(2)}, u32[]{:S(2)}) collective-permute-start(f32[264,128]{1,0:T(8,128)S(1)} %get-tuple-element.44), channel_id=1, source_target_pairs={{0,4},{1,5},{2,6},{3,7},{4,8},{5,9},{6,10},{7,11},{8,12},{9,13},{1... | collective-permute-start | bytes 405512 | tf_op jit(solution)/shard_map/ppermute | solution.py:227
  4.9 1.6 %collective-permute-start = (f32[264,128]{1,0:T(8,128)S(1)}, f32[264,128]{1,0:T(8,128)S(1)}, u32[]{:S(2)}, u32[]{:S(2)}) collective-permute-start(f32[264,128]{1,0:T(8,128)S(1)} %get-tuple-element.44), channel_id=1, source_target_pairs={{0,8},{1,9},{2,10},{3,11},{4,12},{5,13},{6,14},{7,15},{8,16},{9,17... | collective-permute-start | bytes 405512 | tf_op jit(solution)/shard_map/ppermute | solution.py:227
  6.5 0.6 %copy-done.5 = f32[128]{0:T(128)S(1)} copy-done((f32[128]{0:T(128)S(1)}, f32[128]{0:T(128)}, u32[]{:S(2)}) %copy-start.5) | copy-done | bytes 536
  7.2 1.0 %inside.1 = (f32[512,128]{1,0:T(8,128)S(1)}, f32[8,128]{1,0:T(8,128)S(1)}, f32[512,128]{1,0:T(8,128)S(1)}, bf16[512,512]{1,0:T(8,128)(2,1)S(1)}, bf16[512,512]{1...) custom-call(bf16[512,128]{1,0:T(8,128)(2,1)S(1)} %bitcast.15, ...), custom_call_target="tpu_custom_call" | custom-call | flops 100000000 | bytes 3807232 | tf_op jit(solution)/shard_map/inside/pallas_call | solution.py:206
  8.2 4.2 %collective-permute-done.1.refs_1_ = f32[264,128]{1,0:T(8,128)S(1)} collective-permute-done((f32[264,128]{1,0:T(8,128)S(1)}, f32[264,128]{1,0:T(8,128)S(1)}, u32[]{:S(2)}, u32[]{:S(2)}) %collective-permute-start.1) | collective-permute-done | bytes 135200 | tf_op jit(solution)/shard_map/ppermute | solution.py:227
  12.4 0.0 collective-permute-done.refs_0_
  12.4 0.8 %middle.1 = (bf16[512,128]{1,0:T(8,128)(2,1)S(1)}, bf16[512,128]{1,0:T(8,128)(2,1)S(1)}, bf16[512,128]{1,0:T(8,128)(2,1)S(1)}, f32[264,128]{1,0:T(8,128)S(1)}, f32[32,2,128]{2,1,0:T(2,128)S(1)}) custom-call(bf16[512,128]{1,0:T(8,128)(2,1)S(1)} %bitcast.16, bf16[512,256]{1,0:T(8,128)(2,1)S(1)} %get-tuple-element.35.first_queries_ref, ...), custom_call_target="tpu_custom_call" | custom-call | flops 100000000 | bytes 3458048 | tf_op jit(solution)/shard_map/middle/pallas_call | solution.py:206
  13.2 0.1 collective-permute-start.3
  13.3 4.2 %collective-permute-start.2 = (f32[264,128]{1,0:T(8,128)S(1)}, f32[264,128]{1,0:T(8,128)S(1)}, u32[]{:S(2)}, u32[]{:S(2)}) collective-permute-start(f32[264,128]{1,0:T(8,128)S(1)} %get-tuple-element.51), channel_id=1, source_target_pairs={{0,28},{1,29},{2,30},{3,31},{4,0},{5,1},{6,2},{7,3},{8,4},{9,5},{1... | collective-permute-start | bytes 405512 | tf_op jit(solution)/shard_map/ppermute | solution.py:227
  17.5 9.3 %all_to_all.5 = f32[32,2,128]{2,1,0:T(2,128)S(1)} all-to-all(f32[32,2,128]{2,1,0:T(2,128)S(1)} %get-tuple-element.48), channel_id=1, replica_groups=mesh['ctx'=8,'head'=4] {'head','ctx'}, dimensions={0} | all-to-all | bytes 65536 | tf_op jit(solution)/shard_map/all_to_all | solution.py:296
  26.8 0.0 collective-permute-done.3.refs_1_
  26.8 0.0 collective-permute-done.2.refs_0_
  26.8 1.1 %last.1 = (bf16[512,128]{1,0:T(8,128)(2,1)}, bf16[512,128]{1,0:T(8,128)(2,1)}, bf16[512,128]{1,0:T(8,128)(2,1)}, f32[1,128]{1,0:T(1,128)}, f32[1,128]{1,0:T(1,128)}) custom-call(bf16[512,128]{1,0:T(8,128)(2,1)S(1)} %get-tuple-element.45.gnorm_ref, bf16[512,512]{1,0:T(8,128)(2,1)S(1)} %get-tuple-element.46.scores_t_ref, ...), custom_call_target="tpu_custom_call" | custom-call | flops 100000000 | bytes 1881088 | tf_op jit(solution)/shard_map/last/pallas_call | solution.py:206
  (5 shorter events, 0.0 us)
Async XLA Ops:
  0.6 1.0 %copy-start = (bf16[256,2,128]{2,1,0:T(2,128)(2,1)S(1)}, bf16[256,2,128]{2,1,0:T(2,128)(2,1)}, u32[]{:S(2)}) copy-start(bf16[256,2,128]{2,1,0:T(2,128)(2,1)} %param.9) | copy-start | bytes 393220
  0.6 1.0 %copy-start.3 = (s32[256,2,128]{2,1,0:T(2,128)S(1)}, s32[256,2,128]{2,1,0:T(2,128)}, u32[]{:S(2)}) copy-start(s32[256,2,128]{2,1,0:T(2,128)} %param.8) | copy-start | bytes 786436
  0.7 0.7 %copy-start.4 = (s32[256]{0:T(256)S(1)}, s32[256]{0:T(256)}, u32[]{:S(2)}) copy-start(s32[256]{0:T(256)} %param.12) | copy-start | bytes 3076
  0.8 0.7 %copy-start.6 = (f32[128]{0:T(128)S(1)}, f32[128]{0:T(128)}, u32[]{:S(2)}) copy-start(f32[128]{0:T(128)} %param.10) | copy-start | bytes 1540
  1.7 4.8 %copy-start.1 = (bf16[256,2,128]{2,1,0:T(2,128)(2,1)S(1)}, bf16[256,2,128]{2,1,0:T(2,128)(2,1)}, u32[]{:S(2)}) copy-start(bf16[256,2,128]{2,1,0:T(2,128)(2,1)} %param.7) | copy-start | bytes 393220
  1.7 4.8 %copy-start.2 = (bf16[256,2,128]{2,1,0:T(2,128)(2,1)S(1)}, bf16[256,2,128]{2,1,0:T(2,128)(2,1)}, u32[]{:S(2)}) copy-start(bf16[256,2,128]{2,1,0:T(2,128)(2,1)} %param.13) | copy-start | bytes 393220
  1.9 10.4 %collective-permute-start.1 = (f32[264,128]{1,0:T(8,128)S(1)}, f32[264,128]{1,0:T(8,128)S(1)}, u32[]{:S(2)}, u32[]{:S(2)}) collective-permute-start(f32[264,128]{1,0:T(8,128)S(1)} %get-tuple-element.44), channel_id=1, source_target_pairs={{0,4},{1,5},{2,6},{3,7},{4,8},{5,9},{6,10},{7,11},{8,12},{9,13},{1... | collective-permute-start | bytes 405512 | tf_op jit(solution)/shard_map/ppermute | solution.py:227
  4.9 7.5 %collective-permute-start = (f32[264,128]{1,0:T(8,128)S(1)}, f32[264,128]{1,0:T(8,128)S(1)}, u32[]{:S(2)}, u32[]{:S(2)}) collective-permute-start(f32[264,128]{1,0:T(8,128)S(1)} %get-tuple-element.44), channel_id=1, source_target_pairs={{0,8},{1,9},{2,10},{3,11},{4,12},{5,13},{6,14},{7,15},{8,16},{9,17... | collective-permute-start | bytes 405512 | tf_op jit(solution)/shard_map/ppermute | solution.py:227
  6.5 0.7 %copy-start.5 = (f32[128]{0:T(128)S(1)}, f32[128]{0:T(128)}, u32[]{:S(2)}) copy-start(f32[128]{0:T(128)} %param.11) | copy-start | bytes 1540
  13.2 13.6 %collective-permute-start.3 = (f32[264,128]{1,0:T(8,128)S(1)}, f32[264,128]{1,0:T(8,128)S(1)}, u32[]{:S(2)}, u32[]{:S(2)}) collective-permute-start(f32[264,128]{1,0:T(8,128)S(1)} %get-tuple-element.51), channel_id=1, source_target_pairs={{0,25},{1,24},{2,27},{3,26},{4,29},{5,28},{6,31},{7,30},{8,0},{9,1... | collective-permute-start | bytes 405512 | tf_op jit(solution)/shard_map/ppermute | solution.py:227
  13.3 13.5 %collective-permute-start.2 = (f32[264,128]{1,0:T(8,128)S(1)}, f32[264,128]{1,0:T(8,128)S(1)}, u32[]{:S(2)}, u32[]{:S(2)}) collective-permute-start(f32[264,128]{1,0:T(8,128)S(1)} %get-tuple-element.51), channel_id=1, source_target_pairs={{0,28},{1,29},{2,30},{3,31},{4,0},{5,1},{6,2},{7,3},{8,4},{9,5},{1... | collective-permute-start | bytes 405512 | tf_op jit(solution)/shard_map/ppermute | solution.py:227

commit v7 on v6

--- a/solution.py
+++ b/solution.py
@@ -88,8 +88,8 @@
 
 def inside_kernel(
     heads, queries_ref, keys_ref, values_ref, cotangent_ref, gain_ref, ids_ref, last_ref, own_ref,
-    first_ref, head_mark_ref, base_ref, scores_t_ref, mask_ref, values_t_ref, first_queries_ref,
-    first_queries_t_ref, last_keys_ref, upstream_ref, gain_out_ref,
+    head_mark_ref, base_ref, into_values_ref, mask_ref, values_t_ref, first_queries_ref,
+    first_queries_t_ref, upstream_ref, own_first_ref, gain_out_ref,
 ):
     rows = queries_ref.shape[0]
     tokens = ids_ref.shape[1]
@@ -97,8 +97,7 @@
     ids = ids_ref[...].astype(F32)
     head = ids[:, :1]
     in_first = jnp.sum((ids == head).astype(jnp.int32), axis=1, keepdims=True)
-    first = (row_iota(first_ref.shape) < heads * in_first).astype(F32)
-    first_ref[...] = first
+    first = (row_iota(base_ref.shape) < heads * in_first).astype(F32)
     head_mark_ref[...] = jnp.broadcast_to(head, head_mark_ref.shape)
     apart = row_iota((rows, tokens)) - heads * col_iota((rows, tokens))
     down = jnp.sum(
@@ -112,7 +111,7 @@
     allowed_t = (together & (r <= c)).astype(F32).astype(BF16)
     keys = keys_ref[...]
     scores = dot_nt(queries, keys).astype(BF16) * allowed
-    scores_t_ref[...] = dot_nt(keys, queries).astype(BF16) * allowed_t
+    wide = dot_nt(keys, queries).astype(BF16) * allowed_t
     mask_ref[...] = allowed
     values_t_ref[...] = values_ref[...].T
     first_queries = spread_heads(
@@ -120,7 +119,12 @@
     )
     first_queries_ref[...] = first_queries
     first_queries_t_ref[...] = first_queries.T
-    last_keys_ref[...] = spread_heads((keys.astype(F32) * last_ref[...]).astype(BF16), own_ref)
+    into_values_ref[:, :rows] = wide
+    into_values_ref[:, rows:] = spread_heads(
+        (keys.astype(F32) * last_ref[...]).astype(BF16), own_ref
+    )
+    for h in range(heads):
+        own_first_ref[h] = (own_ref[h].astype(F32) * first).astype(BF16)
     gain_out_ref[...] = gain_ref[...]
     upstream_ref[...] = cotangent_ref[...].astype(F32) * gain_ref[...]
     base_ref[...] = queries.astype(F32) + dot_nn(scores, values_ref[...])
@@ -128,15 +132,14 @@
 
 def middle_kernel(
     heads, hops, queries_ref, first_queries_ref, first_queries_t_ref, values_t_ref, cotangent_ref,
-    upstream_ref, base_ref, mask_ref, keys_ref, threshold_ref, gain_ref, first_ref, head_mark_ref,
-    own_ref, *refs,
+    upstream_ref, base_ref, mask_ref, keys_ref, threshold_ref, gain_ref, head_mark_ref,
+    own_first_ref, *refs,
 ):
     received = refs[:hops]
     attended_ref, query_grad_ref, gnorm_ref, back_ref, partial_ref = refs[hops:]
     rows, width = queries_ref.shape
     carried = take_messages(received, head_mark_ref)
     gain = gain_ref[...]
-    first = first_ref[...]
     queries = queries_ref[...]
     mixed = base_ref[...] + dot_nn(first_queries_ref[...], carried)
     cotangent = cotangent_ref[...].astype(F32)
@@ -144,16 +147,26 @@
     square = jnp.mean(mixed * mixed, axis=1, keepdims=True)
     inner = jnp.mean(mixed * upstream, axis=1, keepdims=True)
     ratio = lax.rsqrt(square + 1e-06)
-    gnorm_f = ratio * upstream - mixed * (ratio * ratio * ratio * inner)
-    gnorm = gnorm_f.astype(BF16)
+    gnorm = (ratio * upstream - mixed * (ratio * ratio * ratio * inner)).astype(BF16)
     gnorm_ref[...] = gnorm
-    spread = spread_heads((gnorm_f * first).astype(BF16), own_ref)
+    spread = spread_heads(gnorm, own_first_ref)
     half = rows // 2
     early = dot_nn(gnorm[:half], values_t_ref[:, :half]).astype(BF16) * mask_ref[:half, :half]
     late = dot_nn(gnorm[half:], values_t_ref[...]).astype(BF16) * mask_ref[half:, :]
+    back_states = side_by_side(carried, heads).T
     mixing = jnp.concatenate(
-        [dot_nn(early, keys_ref[:half, :]), dot_nn(late, keys_ref[...])], axis=0
-    ) + dot_nt(spread, side_by_side(carried, heads))
+        [
+            dot_nn(
+                jnp.concatenate([early, spread[:half]], axis=1),
+                jnp.concatenate([keys_ref[:half, :], back_states], axis=0),
+            ),
+            dot_nn(
+                jnp.concatenate([late, spread[half:]], axis=1),
+                jnp.concatenate([keys_ref[...], back_states], axis=0),
+            ),
+        ],
+        axis=0,
+    )
     query_grad_ref[...] = (gnorm.astype(F32) + mixing).astype(BF16)
     normed = mixed * ratio
     attended_ref[...] = (normed * gain).astype(BF16)
@@ -165,7 +178,7 @@
 
 
 def last_kernel(
-    heads, hops, scale, gnorm_ref, scores_t_ref, last_keys_ref, tail_mark_ref, parts_ref,
+    heads, hops, scale, gnorm_ref, into_values_ref, tail_mark_ref, parts_ref,
     attended_ref, query_grad_ref, *refs,
 ):
     received = refs[:hops]
@@ -187,8 +200,8 @@
     gain_ref[...] = jnp.sum(jnp.where(even, 0.0, parts), axis=0, keepdims=True) * scale
     copies[4].start()
     returned = take_messages(received, tail_mark_ref)
-    across = dot_nn(last_keys_ref[...], returned)
-    value_grad_ref[...] = (dot_nn(scores_t_ref[...], gnorm_ref[...]) + across).astype(BF16)
+    sources = jnp.concatenate([gnorm_ref[...], returned], axis=0)
+    value_grad_ref[...] = dot_nn(into_values_ref[...], sources).astype(BF16)
     copies[2].start()
     for copy in copies:
         copy.wait()
@@ -278,18 +291,18 @@
     )
     ahead = neighbours(tail, reach, 1)
     wide = like((rows, heads * width), BF16)
-    first, head_mark, base, scores_t, mask, v_t, first_q, first_q_t, last_k, upstream, gain = call(
+    head_mark, base, into_v, mask, v_t, first_q, first_q_t, upstream, own_first, gain = call(
         functools.partial(inside_kernel, heads),
         "inside",
-        [flat_f, mark, flat_f, square, square, like((width, rows), BF16), wide, like((heads * width, rows), BF16),
-         wide, flat_f, row_f],
+        [mark, flat_f, like((rows, rows + heads * width), BF16), square, like((width, rows), BF16),
+         wide, like((heads * width, rows), BF16), flat_f, like((heads, rows, width), BF16), row_f],
         (q, keys, v, ct, gain, ids, last, own),
     )
     attended, query_grad, gnorm, back, partial = call(
         functools.partial(middle_kernel, heads, len(ahead)),
         "middle",
         [flat_bf, flat_bf, flat_bf, message, like((devices, 2, width), F32)],
-        (q, first_q, first_q_t, v_t, ct, upstream, base, mask, keys, thr, gain, first, head_mark, own,
+        (q, first_q, first_q_t, v_t, ct, upstream, base, mask, keys, thr, gain, head_mark, own_first,
          *ahead),
     )
     behind = neighbours(back, reach, -1)
@@ -299,7 +312,7 @@
         functools.partial(last_kernel, heads, len(behind), scale),
         "last",
         [flat_bf, flat_bf, flat_bf, row_f, row_f],
-        (gnorm, scores_t, last_k, tail_mark, parts.reshape(2 * devices, width), attended, query_grad,
+        (gnorm, into_v, tail_mark, parts.reshape(2 * devices, width), attended, query_grad,
          *behind),
         out_spaces=[HBM] * 5,
         scratch=[pltpu.VMEM((rows, width), BF16), pltpu.VMEM((1, width), F32),

time: 28.1 us -> 28.1 us (level)
  no operation moved by 1% of the time
where the time goes in v7:
time: 28.1 us; the launch traced here: 27.9 us
  blocking collectives  9.32 us (33%)
  starting transfers between devices  8.84 us (31%)
  waiting for transfers between devices  4.19 us (15%)
  Pallas kernels  3.44 us (12%)
  local copies, waits for them, and re-layouts  1.37 us (5%)
  between operations  0.74 us (3%)
    all_to_all x1, blocking collectives, on_device(): parts = lax.all_to_all(partial, ('head', 'ctx'), 0, 0)  9.32 us
    ppermute x4, starting transfers between devices, shifted(): return lax.ppermute(x, ('ctx', 'head'), pairs)  8.84 us
    ppermute x4, waiting for transfers between devices, shifted(): return lax.ppermute(x, ('ctx', 'head'), pairs)  4.19 us
    pallas_call x6, Pallas kernels, call(): pl.pallas_call(kernel, name=name, out_shape=out, in_specs=[in_space] * le...  3.44 us
    unnamed x14, local copies, waits for them, and re-layouts  1.37 us
  transfers between devices with their start and end apart: 4, of which 1 were waited for; matrix products, arithmetic and copies ran while one was open for 0% of the time, Pallas kernels for 4%

profile of v7, /device:TPU:0, one launch (start us, length us, event | category | flops | bytes accessed | tf_op | source)
XLA Modules:
  0.0 27.9 jit_solution(269276899216486142)
XLA Ops:
  0.6 0.0 copy-start
  0.6 0.0 copy-start.3
  0.7 0.1 pattern.1.own_ref
  0.7 0.0 copy-start.4
  0.8 0.0 copy-start.6
  0.8 0.7 %copy-done.4 = s32[256]{0:T(256)S(1)} copy-done((s32[256]{0:T(256)S(1)}, s32[256]{0:T(256)}, u32[]{:S(2)}) %copy-start.4) | copy-done | bytes 1048
  1.5 0.0 copy-done.6
  1.5 0.2 marks.1
  1.7 0.0 copy-start.1
  1.7 0.0 copy-start.2
  1.7 0.2 tail.1
  1.9 3.0 %collective-permute-start.1 = (f32[264,128]{1,0:T(8,128)S(1)}, f32[264,128]{1,0:T(8,128)S(1)}, u32[]{:S(2)}, u32[]{:S(2)}) collective-permute-start(f32[264,128]{1,0:T(8,128)S(1)} %get-tuple-element.43), channel_id=1, source_target_pairs={{0,4},{1,5},{2,6},{3,7},{4,8},{5,9},{6,10},{7,11},{8,12},{9,13},{1... | collective-permute-start | bytes 405512 | tf_op jit(solution)/shard_map/ppermute | solution.py:240
  4.9 1.6 %collective-permute-start = (f32[264,128]{1,0:T(8,128)S(1)}, f32[264,128]{1,0:T(8,128)S(1)}, u32[]{:S(2)}, u32[]{:S(2)}) collective-permute-start(f32[264,128]{1,0:T(8,128)S(1)} %get-tuple-element.43), channel_id=1, source_target_pairs={{0,8},{1,9},{2,10},{3,11},{4,12},{5,13},{6,14},{7,15},{8,16},{9,17... | collective-permute-start | bytes 405512 | tf_op jit(solution)/shard_map/ppermute | solution.py:240
  6.5 0.6 %copy-done.5 = f32[128]{0:T(128)S(1)} copy-done((f32[128]{0:T(128)S(1)}, f32[128]{0:T(128)}, u32[]{:S(2)}) %copy-start.5) | copy-done | bytes 536
  7.2 1.0 %inside.1 = (f32[8,128]{1,0:T(8,128)S(1)}, f32[512,128]{1,0:T(8,128)S(1)}, bf16[512,768]{1,0:T(8,128)(2,1)S(1)}, bf16[512,512]{1,0:T(8,128)(2,1)S(1)}, bf16[128,...) custom-call(bf16[512,128]{1,0:T(8,128)(2,1)S(1)} %bitcast.15, ...), custom_call_target="tpu_custom_call" | custom-call | flops 100000000 | bytes 3807232 | tf_op jit(solution)/shard_map/inside/pallas_call | solution.py:219
  8.2 4.2 %collective-permute-done.1.refs_1_ = f32[264,128]{1,0:T(8,128)S(1)} collective-permute-done((f32[264,128]{1,0:T(8,128)S(1)}, f32[264,128]{1,0:T(8,128)S(1)}, u32[]{:S(2)}, u32[]{:S(2)}) %collective-permute-start.1) | collective-permute-done | bytes 135200 | tf_op jit(solution)/shard_map/ppermute | solution.py:240
  12.4 0.0 collective-permute-done.refs_0_
  12.4 0.8 %middle.1 = (bf16[512,128]{1,0:T(8,128)(2,1)S(1)}, bf16[512,128]{1,0:T(8,128)(2,1)S(1)}, bf16[512,128]{1,0:T(8,128)(2,1)S(1)}, f32[264,128]{1,0:T(8,128)S(1)}, f32[32,2,128]{2,1,0:T(2,128)S(1)}) custom-call(bf16[512,128]{1,0:T(8,128)(2,1)S(1)} %bitcast.16, bf16[512,256]{1,0:T(8,128)(2,1)S(1)} %get-tuple-element.34.first_queries_ref, ...), custom_call_target="tpu_custom_call" | custom-call | flops 100000000 | bytes 3195904 | tf_op jit(solution)/shard_map/middle/pallas_call | solution.py:219
  13.2 0.1 collective-permute-start.3
  13.3 4.2 %collective-permute-start.2 = (f32[264,128]{1,0:T(8,128)S(1)}, f32[264,128]{1,0:T(8,128)S(1)}, u32[]{:S(2)}, u32[]{:S(2)}) collective-permute-start(f32[264,128]{1,0:T(8,128)S(1)} %get-tuple-element.49), channel_id=1, source_target_pairs={{0,28},{1,29},{2,30},{3,31},{4,0},{5,1},{6,2},{7,3},{8,4},{9,5},{1... | collective-permute-start | bytes 405512 | tf_op jit(solution)/shard_map/ppermute | solution.py:240
  17.5 9.3 %all_to_all.5 = f32[32,2,128]{2,1,0:T(2,128)S(1)} all-to-all(f32[32,2,128]{2,1,0:T(2,128)S(1)} %get-tuple-element.46), channel_id=1, replica_groups=mesh['ctx'=8,'head'=4] {'head','ctx'}, dimensions={0} | all-to-all | bytes 65536 | tf_op jit(solution)/shard_map/all_to_all | solution.py:309
  26.8 0.0 collective-permute-done.3.refs_1_
  26.8 0.0 collective-permute-done.2.refs_0_
  26.8 1.1 %last.1 = (bf16[512,128]{1,0:T(8,128)(2,1)}, bf16[512,128]{1,0:T(8,128)(2,1)}, bf16[512,128]{1,0:T(8,128)(2,1)}, f32[1,128]{1,0:T(1,128)}, f32[1,128]{1,0:T(1,128)}) custom-call(bf16[512,128]{1,0:T(8,128)(2,1)S(1)} %get-tuple-element.44.gnorm_ref, bf16[512,768]{1,0:T(8,128)(2,1)S(1)} %get-tuple-element.45.into_values_ref, ...), custom_call_target="tpu_custom_call" | custom-call | flops 100000000 | bytes 1881088 | tf_op jit(solution)/shard_map/last/pallas_call | solution.py:219
  (5 shorter events, 0.0 us)
Async XLA Ops:
  0.6 1.0 %copy-start = (bf16[256,2,128]{2,1,0:T(2,128)(2,1)S(1)}, bf16[256,2,128]{2,1,0:T(2,128)(2,1)}, u32[]{:S(2)}) copy-start(bf16[256,2,128]{2,1,0:T(2,128)(2,1)} %param.9) | copy-start | bytes 393220
  0.6 1.0 %copy-start.3 = (s32[256,2,128]{2,1,0:T(2,128)S(1)}, s32[256,2,128]{2,1,0:T(2,128)}, u32[]{:S(2)}) copy-start(s32[256,2,128]{2,1,0:T(2,128)} %param.8) | copy-start | bytes 786436
  0.7 0.7 %copy-start.4 = (s32[256]{0:T(256)S(1)}, s32[256]{0:T(256)}, u32[]{:S(2)}) copy-start(s32[256]{0:T(256)} %param.12) | copy-start | bytes 3076
  0.8 0.7 %copy-start.6 = (f32[128]{0:T(128)S(1)}, f32[128]{0:T(128)}, u32[]{:S(2)}) copy-start(f32[128]{0:T(128)} %param.10) | copy-start | bytes 1540
  1.7 4.8 %copy-start.1 = (bf16[256,2,128]{2,1,0:T(2,128)(2,1)S(1)}, bf16[256,2,128]{2,1,0:T(2,128)(2,1)}, u32[]{:S(2)}) copy-start(bf16[256,2,128]{2,1,0:T(2,128)(2,1)} %param.7) | copy-start | bytes 393220
  1.7 4.8 %copy-start.2 = (bf16[256,2,128]{2,1,0:T(2,128)(2,1)S(1)}, bf16[256,2,128]{2,1,0:T(2,128)(2,1)}, u32[]{:S(2)}) copy-start(bf16[256,2,128]{2,1,0:T(2,128)(2,1)} %param.13) | copy-start | bytes 393220
  1.9 10.4 %collective-permute-start.1 = (f32[264,128]{1,0:T(8,128)S(1)}, f32[264,128]{1,0:T(8,128)S(1)}, u32[]{:S(2)}, u32[]{:S(2)}) collective-permute-start(f32[264,128]{1,0:T(8,128)S(1)} %get-tuple-element.43), channel_id=1, source_target_pairs={{0,4},{1,5},{2,6},{3,7},{4,8},{5,9},{6,10},{7,11},{8,12},{9,13},{1... | collective-permute-start | bytes 405512 | tf_op jit(solution)/shard_map/ppermute | solution.py:240
  4.9 7.5 %collective-permute-start = (f32[264,128]{1,0:T(8,128)S(1)}, f32[264,128]{1,0:T(8,128)S(1)}, u32[]{:S(2)}, u32[]{:S(2)}) collective-permute-start(f32[264,128]{1,0:T(8,128)S(1)} %get-tuple-element.43), channel_id=1, source_target_pairs={{0,8},{1,9},{2,10},{3,11},{4,12},{5,13},{6,14},{7,15},{8,16},{9,17... | collective-permute-start | bytes 405512 | tf_op jit(solution)/shard_map/ppermute | solution.py:240
  6.5 0.7 %copy-start.5 = (f32[128]{0:T(128)S(1)}, f32[128]{0:T(128)}, u32[]{:S(2)}) copy-start(f32[128]{0:T(128)} %param.11) | copy-start | bytes 1540
  13.2 13.6 %collective-permute-start.3 = (f32[264,128]{1,0:T(8,128)S(1)}, f32[264,128]{1,0:T(8,128)S(1)}, u32[]{:S(2)}, u32[]{:S(2)}) collective-permute-start(f32[264,128]{1,0:T(8,128)S(1)} %get-tuple-element.49), channel_id=1, source_target_pairs={{0,25},{1,24},{2,27},{3,26},{4,29},{5,28},{6,31},{7,30},{8,0},{9,1... | collective-permute-start | bytes 405512 | tf_op jit(solution)/shard_map/ppermute | solution.py:240
  13.3 13.5 %collective-permute-start.2 = (f32[264,128]{1,0:T(8,128)S(1)}, f32[264,128]{1,0:T(8,128)S(1)}, u32[]{:S(2)}, u32[]{:S(2)}) collective-permute-start(f32[264,128]{1,0:T(8,128)S(1)} %get-tuple-element.49), channel_id=1, source_target_pairs={{0,28},{1,29},{2,30},{3,31},{4,0},{5,1},{6,2},{7,3},{8,4},{9,5},{1... | collective-permute-start | bytes 405512 | tf_op jit(solution)/shard_map/ppermute | solution.py:240

commit v8 on v7

--- a/solution.py
+++ b/solution.py
@@ -60,16 +60,17 @@
     return jnp.concatenate([state[h * count : (h + 1) * count] for h in range(heads)], axis=1)
 
 
-def pattern_kernel(heads, own_ref):
+def opening_kernel(zero_ref):
+    zero_ref[...] = jnp.zeros_like(zero_ref)
+
+
+def marks_kernel(
+    heads, ids_ref, threshold_ref, zero_ref, last_ref, tail_mark_ref, threshold_out_ref, own_ref
+):
+    threshold_out_ref[...] = threshold_ref[...]
     head = lax.rem(row_iota(own_ref.shape[1:]), heads)
     for h in range(heads):
         own_ref[h] = (head == h).astype(BF16)
-
-
-def marks_kernel(
-    heads, ids_ref, threshold_ref, last_ref, tail_mark_ref, threshold_out_ref
-):
-    threshold_out_ref[...] = threshold_ref[...]
     ids = ids_ref[...]
     tail = ids[:, ids.shape[1] - 1 :]
     before_last = jnp.sum((ids != tail).astype(jnp.int32), axis=1, keepdims=True)
@@ -271,16 +272,12 @@
 
     flat_f = like((rows, width), F32)
     square = like((rows, rows), BF16)
-    (own,) = call(
-        functools.partial(pattern_kernel, heads),
-        "pattern",
-        [like((heads, rows, width), BF16)],
-        (),
-        flops=4 * 10**9,
+    (zero,) = call(
+        opening_kernel, "opening", [like((8, 128), F32)], (), flops=4 * 10**9
     )
     mark = like((MARK_ROWS, width), F32)
-    last, tail_mark, thr = call(
-        functools.partial(marks_kernel, heads), "marks", [flat_f, mark, row_f], (ids, thr),
+    last, tail_mark, thr, own = call(
+        functools.partial(marks_kernel, heads), "marks", [flat_f, mark, row_f, like((heads, rows, width), BF16)], (ids, thr, zero),
         flops=1, size=1,
     )
     tail, keys = call(

time: 28.1 us -> 28.1 us (level)
  no operation moved by 1% of the time
where the time goes in v8:
time: 28.1 us; the launch traced here: 27.9 us
  blocking collectives  9.32 us (33%)
  starting transfers between devices  8.84 us (31%)
  waiting for transfers between devices  4.19 us (15%)
  Pallas kernels  3.38 us (12%)
  local copies, waits for them, and re-layouts  1.45 us (5%)
  between operations  0.72 us (3%)
    all_to_all x1, blocking collectives, on_device(): parts = lax.all_to_all(partial, ('head', 'ctx'), 0, 0)  9.32 us
    ppermute x4, starting transfers between devices, shifted(): return lax.ppermute(x, ('ctx', 'head'), pairs)  8.84 us
    ppermute x4, waiting for transfers between devices, shifted(): return lax.ppermute(x, ('ctx', 'head'), pairs)  4.19 us
    pallas_call x6, Pallas kernels, call(): pl.pallas_call(kernel, name=name, out_shape=out, in_specs=[in_space] * le...  3.38 us
    unnamed x14, local copies, waits for them, and re-layouts  1.45 us
  transfers between devices with their start and end apart: 4, of which 1 were waited for; matrix products, arithmetic and copies ran while one was open for 0% of the time, Pallas kernels for 4%

profile of v8, /device:TPU:0, one launch (start us, length us, event | category | flops | bytes accessed | tf_op | source)
XLA Modules:
  0.0 27.9 jit_solution(9711247570661538640)
XLA Ops:
  0.6 0.0 copy-start
  0.6 0.0 copy-start.3
  0.7 0.0 copy-start.4
  0.7 0.0 copy-start.6
  0.7 0.7 %copy-done.4 = s32[256]{0:T(256)S(1)} copy-done((s32[256]{0:T(256)S(1)}, s32[256]{0:T(256)}, u32[]{:S(2)}) %copy-start.4) | copy-done | bytes 1048
  1.4 0.0 copy-done.6
  1.4 0.2 marks.1
  1.6 0.0 copy-done
  1.6 0.1 copy-done.3
  1.7 0.2 tail.1
  1.9 3.0 %collective-permute-start.1 = (f32[264,128]{1,0:T(8,128)S(1)}, f32[264,128]{1,0:T(8,128)S(1)}, u32[]{:S(2)}, u32[]{:S(2)}) collective-permute-start(f32[264,128]{1,0:T(8,128)S(1)} %get-tuple-element.45), channel_id=1, source_target_pairs={{0,4},{1,5},{2,6},{3,7},{4,8},{5,9},{6,10},{7,11},{8,12},{9,13},{1... | collective-permute-start | bytes 405512 | tf_op jit(solution)/shard_map/ppermute | solution.py:241
  4.9 1.6 %collective-permute-start = (f32[264,128]{1,0:T(8,128)S(1)}, f32[264,128]{1,0:T(8,128)S(1)}, u32[]{:S(2)}, u32[]{:S(2)}) collective-permute-start(f32[264,128]{1,0:T(8,128)S(1)} %get-tuple-element.45), channel_id=1, source_target_pairs={{0,8},{1,9},{2,10},{3,11},{4,12},{5,13},{6,14},{7,15},{8,16},{9,17... | collective-permute-start | bytes 405512 | tf_op jit(solution)/shard_map/ppermute | solution.py:241
  6.5 0.0 copy-done.2
  6.5 0.6 %copy-done.5 = f32[128]{0:T(128)S(1)} copy-done((f32[128]{0:T(128)S(1)}, f32[128]{0:T(128)}, u32[]{:S(2)}) %copy-start.5) | copy-done | bytes 536
  7.2 1.0 %inside.1 = (f32[8,128]{1,0:T(8,128)S(1)}, f32[512,128]{1,0:T(8,128)S(1)}, bf16[512,768]{1,0:T(8,128)(2,1)S(1)}, bf16[512,512]{1,0:T(8,128)(2,1)S(1)}, bf16[128,...) custom-call(bf16[512,128]{1,0:T(8,128)(2,1)S(1)} %bitcast.15, ...), custom_call_target="tpu_custom_call" | custom-call | flops 100000000 | bytes 3807232 | tf_op jit(solution)/shard_map/inside/pallas_call | solution.py:220
  8.2 4.2 %collective-permute-done.1.refs_1_ = f32[264,128]{1,0:T(8,128)S(1)} collective-permute-done((f32[264,128]{1,0:T(8,128)S(1)}, f32[264,128]{1,0:T(8,128)S(1)}, u32[]{:S(2)}, u32[]{:S(2)}) %collective-permute-start.1) | collective-permute-done | bytes 135200 | tf_op jit(solution)/shard_map/ppermute | solution.py:241
  12.4 0.0 collective-permute-done.refs_0_
  12.4 0.8 %middle.1 = (bf16[512,128]{1,0:T(8,128)(2,1)S(1)}, bf16[512,128]{1,0:T(8,128)(2,1)S(1)}, bf16[512,128]{1,0:T(8,128)(2,1)S(1)}, f32[264,128]{1,0:T(8,128)S(1)}, f32[32,2,128]{2,1,0:T(2,128)S(1)}) custom-call(bf16[512,128]{1,0:T(8,128)(2,1)S(1)} %bitcast.16, bf16[512,256]{1,0:T(8,128)(2,1)S(1)} %get-tuple-element.36.first_queries_ref, ...), custom_call_target="tpu_custom_call" | custom-call | flops 100000000 | bytes 3195904 | tf_op jit(solution)/shard_map/middle/pallas_call | solution.py:220
  13.2 0.1 collective-permute-start.3
  13.3 4.2 %collective-permute-start.2 = (f32[264,128]{1,0:T(8,128)S(1)}, f32[264,128]{1,0:T(8,128)S(1)}, u32[]{:S(2)}, u32[]{:S(2)}) collective-permute-start(f32[264,128]{1,0:T(8,128)S(1)} %get-tuple-element.51), channel_id=1, source_target_pairs={{0,28},{1,29},{2,30},{3,31},{4,0},{5,1},{6,2},{7,3},{8,4},{9,5},{1... | collective-permute-start | bytes 405512 | tf_op jit(solution)/shard_map/ppermute | solution.py:241
  17.5 9.3 %all_to_all.5 = f32[32,2,128]{2,1,0:T(2,128)S(1)} all-to-all(f32[32,2,128]{2,1,0:T(2,128)S(1)} %get-tuple-element.48), channel_id=1, replica_groups=mesh['ctx'=8,'head'=4] {'head','ctx'}, dimensions={0} | all-to-all | bytes 65536 | tf_op jit(solution)/shard_map/all_to_all | solution.py:306
  26.8 0.0 collective-permute-done.3.refs_1_
  26.8 0.0 collective-permute-done.2.refs_0_
  26.8 1.1 %last.1 = (bf16[512,128]{1,0:T(8,128)(2,1)}, bf16[512,128]{1,0:T(8,128)(2,1)}, bf16[512,128]{1,0:T(8,128)(2,1)}, f32[1,128]{1,0:T(1,128)}, f32[1,128]{1,0:T(1,128)}) custom-call(bf16[512,128]{1,0:T(8,128)(2,1)S(1)} %get-tuple-element.46.gnorm_ref, bf16[512,768]{1,0:T(8,128)(2,1)S(1)} %get-tuple-element.47.into_values_ref, ...), custom_call_target="tpu_custom_call" | custom-call | flops 100000000 | bytes 1881088 | tf_op jit(solution)/shard_map/last/pallas_call | solution.py:220
  (5 shorter events, 0.0 us)
Async XLA Ops:
  0.6 1.0 %copy-start = (bf16[256,2,128]{2,1,0:T(2,128)(2,1)S(1)}, bf16[256,2,128]{2,1,0:T(2,128)(2,1)}, u32[]{:S(2)}) copy-start(bf16[256,2,128]{2,1,0:T(2,128)(2,1)} %param.9) | copy-start | bytes 393220
  0.6 1.0 %copy-start.3 = (s32[256,2,128]{2,1,0:T(2,128)S(1)}, s32[256,2,128]{2,1,0:T(2,128)}, u32[]{:S(2)}) copy-start(s32[256,2,128]{2,1,0:T(2,128)} %param.8) | copy-start | bytes 786436
  0.7 0.7 %copy-start.4 = (s32[256]{0:T(256)S(1)}, s32[256]{0:T(256)}, u32[]{:S(2)}) copy-start(s32[256]{0:T(256)} %param.12) | copy-start | bytes 3076
  0.7 0.7 %copy-start.6 = (f32[128]{0:T(128)S(1)}, f32[128]{0:T(128)}, u32[]{:S(2)}) copy-start(f32[128]{0:T(128)} %param.10) | copy-start | bytes 1540
  1.7 4.8 %copy-start.1 = (bf16[256,2,128]{2,1,0:T(2,128)(2,1)S(1)}, bf16[256,2,128]{2,1,0:T(2,128)(2,1)}, u32[]{:S(2)}) copy-start(bf16[256,2,128]{2,1,0:T(2,128)(2,1)} %param.7) | copy-start | bytes 393220
  1.7 4.8 %copy-start.2 = (bf16[256,2,128]{2,1,0:T(2,128)(2,1)S(1)}, bf16[256,2,128]{2,1,0:T(2,128)(2,1)}, u32[]{:S(2)}) copy-start(bf16[256,2,128]{2,1,0:T(2,128)(2,1)} %param.13) | copy-start | bytes 393220
  1.9 10.4 %collective-permute-start.1 = (f32[264,128]{1,0:T(8,128)S(1)}, f32[264,128]{1,0:T(8,128)S(1)}, u32[]{:S(2)}, u32[]{:S(2)}) collective-permute-start(f32[264,128]{1,0:T(8,128)S(1)} %get-tuple-element.45), channel_id=1, source_target_pairs={{0,4},{1,5},{2,6},{3,7},{4,8},{5,9},{6,10},{7,11},{8,12},{9,13},{1... | collective-permute-start | bytes 405512 | tf_op jit(solution)/shard_map/ppermute | solution.py:241
  4.9 7.5 %collective-permute-start = (f32[264,128]{1,0:T(8,128)S(1)}, f32[264,128]{1,0:T(8,128)S(1)}, u32[]{:S(2)}, u32[]{:S(2)}) collective-permute-start(f32[264,128]{1,0:T(8,128)S(1)} %get-tuple-element.45), channel_id=1, source_target_pairs={{0,8},{1,9},{2,10},{3,11},{4,12},{5,13},{6,14},{7,15},{8,16},{9,17... | collective-permute-start | bytes 405512 | tf_op jit(solution)/shard_map/ppermute | solution.py:241
  6.5 0.7 %copy-start.5 = (f32[128]{0:T(128)S(1)}, f32[128]{0:T(128)}, u32[]{:S(2)}) copy-start(f32[128]{0:T(128)} %param.11) | copy-start | bytes 1540
  13.2 13.6 %collective-permute-start.3 = (f32[264,128]{1,0:T(8,128)S(1)}, f32[264,128]{1,0:T(8,128)S(1)}, u32[]{:S(2)}, u32[]{:S(2)}) collective-permute-start(f32[264,128]{1,0:T(8,128)S(1)} %get-tuple-element.51), channel_id=1, source_target_pairs={{0,25},{1,24},{2,27},{3,26},{4,29},{5,28},{6,31},{7,30},{8,0},{9,1... | collective-permute-start | bytes 405512 | tf_op jit(solution)/shard_map/ppermute | solution.py:241
  13.3 13.5 %collective-permute-start.2 = (f32[264,128]{1,0:T(8,128)S(1)}, f32[264,128]{1,0:T(8,128)S(1)}, u32[]{:S(2)}, u32[]{:S(2)}) collective-permute-start(f32[264,128]{1,0:T(8,128)S(1)} %get-tuple-element.51), channel_id=1, source_target_pairs={{0,28},{1,29},{2,30},{3,31},{4,0},{5,1},{6,2},{7,3},{8,4},{9,5},{1... | collective-permute-start | bytes 405512 | tf_op jit(solution)/shard_map/ppermute | solution.py:241

commit v9 on v6

--- a/solution.py
+++ b/solution.py
@@ -222,7 +222,10 @@
         for lane in range(lanes):
             wraps = not 0 <= block + by < count
             swap = wraps and abs(by) == 2 and lanes % 2 == 0
-            to = (block + by) % count * lanes + (lane ^ 1 if swap else lane)
+            target = (block + by) % count
+            if swap and by == 2 and count % 2 == 0:
+                target = target ^ 1
+            to = target * lanes + (lane ^ 1 if swap else lane)
             pairs.append((block * lanes + lane, to))
     return lax.ppermute(x, ("ctx", "head"), pairs)
 

time: 28.1 us -> 28.2 us (level)
  waiting for transfers between devices: 4.22 us -> 5.45 us
  starting transfers between devices: 8.84 us -> 7.61 us
    ppermute x4, waiting for transfers between devices: 4.22 us -> 5.45 us  [shifted(): return lax.ppermute(x, ('ctx', 'head'), pairs)]
    ppermute x4, starting transfers between devices: 8.84 us -> 7.61 us  [shifted(): return lax.ppermute(x, ('ctx', 'head'), pairs)]
  transfers between devices with their start and end apart: 4 -> 4, of which waited for: 1 -> 2; matrix products, arithmetic and copies ran while one was open for 0% -> 0% of each run, Pallas kernels for 4% -> 4%
where the time goes in v9:
time: 28.2 us; the launch traced here: 28.1 us
  blocking collectives  9.43 us (33%)
  starting transfers between devices  7.61 us (27%)
  waiting for transfers between devices  5.45 us (19%)
  Pallas kernels  3.45 us (12%)
  local copies, waits for them, and re-layouts  1.37 us (5%)
  between operations  0.74 us (3%)
    all_to_all x1, blocking collectives, on_device(): parts = lax.all_to_all(partial, ('head', 'ctx'), 0, 0)  9.43 us
    ppermute x4, starting transfers between devices, shifted(): return lax.ppermute(x, ('ctx', 'head'), pairs)  7.61 us
    ppermute x4, waiting for transfers between devices, shifted(): return lax.ppermute(x, ('ctx', 'head'), pairs)  5.45 us
    pallas_call x6, Pallas kernels, call(): pl.pallas_call(kernel, name=name, out_shape=out, in_specs=[in_space] * le...  3.45 us
    unnamed x14, local copies, waits for them, and re-layouts  1.37 us
  transfers between devices with their start and end apart: 4, of which 2 were waited for; matrix products, arithmetic and copies ran while one was open for 0% of the time, Pallas kernels for 4%

profile of v9, /device:TPU:0, one launch (start us, length us, event | category | flops | bytes accessed | tf_op | source)
XLA Modules:
  0.0 28.1 jit_solution(3981347251515624340)
XLA Ops:
  0.6 0.0 copy-start
  0.6 0.0 copy-start.3
  0.7 0.1 pattern.1.own_ref
  0.7 0.0 copy-start.4
  0.8 0.0 copy-start.6
  0.8 0.7 %copy-done.4 = s32[256]{0:T(256)S(1)} copy-done((s32[256]{0:T(256)S(1)}, s32[256]{0:T(256)}, u32[]{:S(2)}) %copy-start.4) | copy-done | bytes 1048
  1.5 0.0 copy-done.6
  1.5 0.2 marks.1
  1.7 0.0 copy-start.1
  1.7 0.0 copy-start.2
  1.7 0.2 tail.1
  1.9 3.0 %collective-permute-start.1 = (f32[264,128]{1,0:T(8,128)S(1)}, f32[264,128]{1,0:T(8,128)S(1)}, u32[]{:S(2)}, u32[]{:S(2)}) collective-permute-start(f32[264,128]{1,0:T(8,128)S(1)} %get-tuple-element.44), channel_id=1, source_target_pairs={{0,4},{1,5},{2,6},{3,7},{4,8},{5,9},{6,10},{7,11},{8,12},{9,13},{1... | collective-permute-start | bytes 405512 | tf_op jit(solution)/shard_map/ppermute | solution.py:230
  4.9 1.6 %collective-permute-start = (f32[264,128]{1,0:T(8,128)S(1)}, f32[264,128]{1,0:T(8,128)S(1)}, u32[]{:S(2)}, u32[]{:S(2)}) collective-permute-start(f32[264,128]{1,0:T(8,128)S(1)} %get-tuple-element.44), channel_id=1, source_target_pairs={{0,8},{1,9},{2,10},{3,11},{4,12},{5,13},{6,14},{7,15},{8,16},{9,17... | collective-permute-start | bytes 405512 | tf_op jit(solution)/shard_map/ppermute | solution.py:230
  6.5 0.6 %copy-done.5 = f32[128]{0:T(128)S(1)} copy-done((f32[128]{0:T(128)S(1)}, f32[128]{0:T(128)}, u32[]{:S(2)}) %copy-start.5) | copy-done | bytes 536
  7.2 1.0 %inside.1 = (f32[512,128]{1,0:T(8,128)S(1)}, f32[8,128]{1,0:T(8,128)S(1)}, f32[512,128]{1,0:T(8,128)S(1)}, bf16[512,512]{1,0:T(8,128)(2,1)S(1)}, bf16[512,512]{1...) custom-call(bf16[512,128]{1,0:T(8,128)(2,1)S(1)} %bitcast.15, ...), custom_call_target="tpu_custom_call" | custom-call | flops 100000000 | bytes 3807232 | tf_op jit(solution)/shard_map/inside/pallas_call | solution.py:206
  8.2 4.2 %collective-permute-done.1.refs_1_ = f32[264,128]{1,0:T(8,128)S(1)} collective-permute-done((f32[264,128]{1,0:T(8,128)S(1)}, f32[264,128]{1,0:T(8,128)S(1)}, u32[]{:S(2)}, u32[]{:S(2)}) %collective-permute-start.1) | collective-permute-done | bytes 135200 | tf_op jit(solution)/shard_map/ppermute | solution.py:230
  12.4 1.2 %collective-permute-done.refs_0_ = f32[264,128]{1,0:T(8,128)S(1)} collective-permute-done((f32[264,128]{1,0:T(8,128)S(1)}, f32[264,128]{1,0:T(8,128)S(1)}, u32[]{:S(2)}, u32[]{:S(2)}) %collective-permute-start) | collective-permute-done | bytes 135200 | tf_op jit(solution)/shard_map/ppermute | solution.py:230
  13.6 0.8 %middle.1 = (bf16[512,128]{1,0:T(8,128)(2,1)S(1)}, bf16[512,128]{1,0:T(8,128)(2,1)S(1)}, bf16[512,128]{1,0:T(8,128)(2,1)S(1)}, f32[264,128]{1,0:T(8,128)S(1)}, f32[32,2,128]{2,1,0:T(2,128)S(1)}) custom-call(bf16[512,128]{1,0:T(8,128)(2,1)S(1)} %bitcast.16, bf16[512,256]{1,0:T(8,128)(2,1)S(1)} %get-tuple-element.35.first_queries_ref, ...), custom_call_target="tpu_custom_call" | custom-call | flops 100000000 | bytes 3458048 | tf_op jit(solution)/shard_map/middle/pallas_call | solution.py:206
  14.5 0.1 collective-permute-start.3
  14.5 3.0 %collective-permute-start.2 = (f32[264,128]{1,0:T(8,128)S(1)}, f32[264,128]{1,0:T(8,128)S(1)}, u32[]{:S(2)}, u32[]{:S(2)}) collective-permute-start(f32[264,128]{1,0:T(8,128)S(1)} %get-tuple-element.51), channel_id=1, source_target_pairs={{0,28},{1,29},{2,30},{3,31},{4,0},{5,1},{6,2},{7,3},{8,4},{9,5},{1... | collective-permute-start | bytes 405512 | tf_op jit(solution)/shard_map/ppermute | solution.py:230
  17.5 9.4 %all_to_all.5 = f32[32,2,128]{2,1,0:T(2,128)S(1)} all-to-all(f32[32,2,128]{2,1,0:T(2,128)S(1)} %get-tuple-element.48), channel_id=1, replica_groups=mesh['ctx'=8,'head'=4] {'head','ctx'}, dimensions={0} | all-to-all | bytes 65536 | tf_op jit(solution)/shard_map/all_to_all | solution.py:299
  27.0 0.0 collective-permute-done.3.refs_1_
  27.0 0.0 collective-permute-done.2.refs_0_
  27.0 1.1 %last.1 = (bf16[512,128]{1,0:T(8,128)(2,1)}, bf16[512,128]{1,0:T(8,128)(2,1)}, bf16[512,128]{1,0:T(8,128)(2,1)}, f32[1,128]{1,0:T(1,128)}, f32[1,128]{1,0:T(1,128)}) custom-call(bf16[512,128]{1,0:T(8,128)(2,1)S(1)} %get-tuple-element.45.gnorm_ref, bf16[512,512]{1,0:T(8,128)(2,1)S(1)} %get-tuple-element.46.scores_t_ref, ...), custom_call_target="tpu_custom_call" | custom-call | flops 100000000 | bytes 1881088 | tf_op jit(solution)/shard_map/last/pallas_call | solution.py:206
  (5 shorter events, 0.0 us)
Async XLA Ops:
  0.6 1.0 %copy-start = (bf16[256,2,128]{2,1,0:T(2,128)(2,1)S(1)}, bf16[256,2,128]{2,1,0:T(2,128)(2,1)}, u32[]{:S(2)}) copy-start(bf16[256,2,128]{2,1,0:T(2,128)(2,1)} %param.9) | copy-start | bytes 393220
  0.6 1.0 %copy-start.3 = (s32[256,2,128]{2,1,0:T(2,128)S(1)}, s32[256,2,128]{2,1,0:T(2,128)}, u32[]{:S(2)}) copy-start(s32[256,2,128]{2,1,0:T(2,128)} %param.8) | copy-start | bytes 786436
  0.7 0.7 %copy-start.4 = (s32[256]{0:T(256)S(1)}, s32[256]{0:T(256)}, u32[]{:S(2)}) copy-start(s32[256]{0:T(256)} %param.12) | copy-start | bytes 3076
  0.8 0.7 %copy-start.6 = (f32[128]{0:T(128)S(1)}, f32[128]{0:T(128)}, u32[]{:S(2)}) copy-start(f32[128]{0:T(128)} %param.10) | copy-start | bytes 1540
  1.7 4.8 %copy-start.1 = (bf16[256,2,128]{2,1,0:T(2,128)(2,1)S(1)}, bf16[256,2,128]{2,1,0:T(2,128)(2,1)}, u32[]{:S(2)}) copy-start(bf16[256,2,128]{2,1,0:T(2,128)(2,1)} %param.7) | copy-start | bytes 393220
  1.7 4.8 %copy-start.2 = (bf16[256,2,128]{2,1,0:T(2,128)(2,1)S(1)}, bf16[256,2,128]{2,1,0:T(2,128)(2,1)}, u32[]{:S(2)}) copy-start(bf16[256,2,128]{2,1,0:T(2,128)(2,1)} %param.13) | copy-start | bytes 393220
  1.9 10.4 %collective-permute-start.1 = (f32[264,128]{1,0:T(8,128)S(1)}, f32[264,128]{1,0:T(8,128)S(1)}, u32[]{:S(2)}, u32[]{:S(2)}) collective-permute-start(f32[264,128]{1,0:T(8,128)S(1)} %get-tuple-element.44), channel_id=1, source_target_pairs={{0,4},{1,5},{2,6},{3,7},{4,8},{5,9},{6,10},{7,11},{8,12},{9,13},{1... | collective-permute-start | bytes 405512 | tf_op jit(solution)/shard_map/ppermute | solution.py:230
  4.9 8.7 %collective-permute-start = (f32[264,128]{1,0:T(8,128)S(1)}, f32[264,128]{1,0:T(8,128)S(1)}, u32[]{:S(2)}, u32[]{:S(2)}) collective-permute-start(f32[264,128]{1,0:T(8,128)S(1)} %get-tuple-element.44), channel_id=1, source_target_pairs={{0,8},{1,9},{2,10},{3,11},{4,12},{5,13},{6,14},{7,15},{8,16},{9,17... | collective-permute-start | bytes 405512 | tf_op jit(solution)/shard_map/ppermute | solution.py:230
  6.5 0.7 %copy-start.5 = (f32[128]{0:T(128)S(1)}, f32[128]{0:T(128)}, u32[]{:S(2)}) copy-start(f32[128]{0:T(128)} %param.11) | copy-start | bytes 1540
  14.5 12.5 %collective-permute-start.3 = (f32[264,128]{1,0:T(8,128)S(1)}, f32[264,128]{1,0:T(8,128)S(1)}, u32[]{:S(2)}, u32[]{:S(2)}) collective-permute-start(f32[264,128]{1,0:T(8,128)S(1)} %get-tuple-element.51), channel_id=1, source_target_pairs={{0,25},{1,24},{2,27},{3,26},{4,29},{5,28},{6,31},{7,30},{8,0},{9,1... | collective-permute-start | bytes 405512 | tf_op jit(solution)/shard_map/ppermute | solution.py:230
  14.5 12.4 %collective-permute-start.2 = (f32[264,128]{1,0:T(8,128)S(1)}, f32[264,128]{1,0:T(8,128)S(1)}, u32[]{:S(2)}, u32[]{:S(2)}) collective-permute-start(f32[264,128]{1,0:T(8,128)S(1)} %get-tuple-element.51), channel_id=1, source_target_pairs={{0,28},{1,29},{2,30},{3,31},{4,0},{5,1},{6,2},{7,3},{8,4},{9,5},{1... | collective-permute-start | bytes 405512 | tf_op jit(solution)/shard_map/ppermute | solution.py:230
